TPU v7x, 32 devices: a whole 2x2x4 slice. The times are simulated.
32 devices in a mesh: row: 4 (over x, core), col: 8 (over z, y).
Axes of the slice: x: 2, y: 2, z: 4, core: 2. Of those that a mesh axis runs over, the one named last changes fastest.
Arguments:
- word_vecs: bfloat16 [32, 4, 1024, 256], P('col', 'row'), may hold values from -1.5 to 1.5
- ctx_vecs: bfloat16 [16, 8, 1024, 256], P('row', 'col'), may hold values from -1.5 to 1.5
- tile_rows: int32 [4, 8, 4], P('row'), may hold values from 0 to 31, as said below
- tile_cols: int32 [4, 8, 4], P(None, 'col'), may hold values from 0 to 15, as said below
- tile_count: int32 [4, 8], replicated, may hold values from 3 to 4
- counts: bfloat16 [4, 8, 4, 1024, 1024], P('row', 'col'), may hold values from 0 to 64
- row_sums: int32 [4, 8, 4, 1024], P('row', 'col'), may hold values from 2000 to 19999
- col_sums: int32 [4, 8, 4, 1024], P('row', 'col'), may hold values from 2000 to 19999
Outputs:
- new_words: bfloat16 [32, 4, 1024, 256], P('col', 'row')
- new_contexts: bfloat16 [16, 8, 1024, 256], P('row', 'col')
Inputs may be any that keep to these rules, and one draw needn't show every extreme that they name: On one device (r, c), the values tile_rows[r, c, t] // 4 of its 4 slots are all different. On one device (r, c), the values tile_cols[r, c, t] // 4 of its 4 slots are all different.
All inputs are finite; a program needn't handle non-finite values.
Results may differ from a plain program's by a relative error of at most 0.0032.
Values may be sent and summed in bfloat16 or wider, within the bound.
No kernel may reach another device: no remote copies, remote signals or barrier semaphores. Data moves between devices by JAX's collectives and lax.ppermute only.
A program may use at most 192 MiB of HBM per device.

v0:
```python
import functools

import jax
import jax.numpy as jnp
from jax import lax
from jax.experimental import pallas as pl
from jax.experimental.pallas import tpu as pltpu
from jax.sharding import PartitionSpec as P

shift_term = 16.0
learn_rate = 0.005
chunks = 2
bf16, f32, i32 = jnp.bfloat16, jnp.float32, jnp.int32
ANY = pl.BlockSpec(memory_space=pl.ANY)
SMEM = pl.BlockSpec(memory_space=pltpu.SMEM)
VMEM = pl.BlockSpec(memory_space=pltpu.VMEM)
big = pltpu.CompilerParams(vmem_limit_bytes=40 * 1024 * 1024)


def swap(x, axis, shift):
    size = lax.axis_size(axis)
    return lax.ppermute(x, axis, [(i, i ^ shift) for i in range(size)])


def bits_set(v):
    srl = lax.shift_right_logical
    v = v - (srl(v, 1) & 0x55555555)
    v = (v & 0x33333333) + (srl(v, 2) & 0x33333333)
    v = (v + srl(v, 4)) & 0x0F0F0F0F
    return srl(v * 0x01010101, 24)


class Sizes:
    def __init__(self, word_vecs, counts):
        self.cols = lax.axis_size("col")
        self.rows = lax.axis_size("row")
        self.half = self.cols // 2
        self.blocks = word_vecs.shape[0]
        self.block, self.dim = word_vecs.shape[2:]
        self.slots = counts.shape[2]
        self.pool = self.half * self.blocks
        self.part = self.block // self.half
        self.step = self.part // chunks
        self.at_send = 8
        self.at_rank = self.at_send + self.pool
        self.at_fetch = self.at_rank + self.pool
        self.at_live = self.at_fetch + self.half * self.slots
        self.table = self.at_live + self.half * self.slots


def table_kernel(z, me_ref, lists_ref, count_ref, out_ref):
    own_row, own_col = me_ref[0], me_ref[1]
    size = z.pool

    def named_across(s):
        row = own_row ^ s

        def visit(c, masks):
            low, high = masks
            for t in range(z.slots):
                a = lists_ref[s, c * z.slots + t]
                side = (a >= size).astype(i32)
                use = jnp.logical_and(t < count_ref[row, c], side != (c >= z.half).astype(i32))
                bit = jnp.where(use, jnp.int32(1) << (a - side * size), 0)
                low = low | jnp.where(side == 0, bit, 0)
                high = high | jnp.where(side == 1, bit, 0)
            return (low, high)

        return lax.fori_loop(0, z.cols, visit, (jnp.int32(0), jnp.int32(0)))

    low, high = named_across(0)

    def most(s, top):
        a, b = named_across(s)
        return jnp.maximum(top, jnp.maximum(bits_set(a), bits_set(b)))

    out_ref[0] = lax.fori_loop(
        1, z.rows, most, jnp.maximum(bits_set(low), bits_set(high))
    )
    side = (own_col >= z.half).astype(i32)
    place = own_col - side * z.half
    out_mask = jnp.where(side == 0, low, high)
    in_mask = jnp.where(side == 0, high, low)
    turn = place * z.blocks

    def clear(p, none):
        out_ref[z.at_send + p] = 0
        return none

    lax.fori_loop(0, size, clear, 0)

    def rank(p, none):
        bit = jnp.int32(1) << p
        r = bits_set(out_mask & (bit - 1))
        used = (out_mask & bit) != 0
        out_ref[z.at_rank + (p ^ turn)] = jnp.where(used, r, -1)

        @pl.when(used)
        def _():
            out_ref[z.at_send + r] = p ^ turn

        return none

    lax.fori_loop(0, size, rank, 0)

    def fetch(s, none):
        c = side * z.half + (place ^ s)
        for t in range(z.slots):
            a = lists_ref[0, c * z.slots + t]
            there = (a >= size).astype(i32)
            p = a - there * size
            live = t < count_ref[own_row, c]
            lane = size + bits_set(in_mask & ((jnp.int32(1) << p) - 1))
            spot = jnp.where(there == side, p ^ turn, lane)
            out_ref[z.at_fetch + s * z.slots + t] = jnp.where(live, spot, 0)
            out_ref[z.at_live + s * z.slots + t] = live.astype(i32)
        return none

    lax.fori_loop(0, z.half, fetch, 0)


def make_table(z, me, lists, tile_count):
    return pl.pallas_call(
        functools.partial(table_kernel, z),
        out_shape=jax.ShapeDtypeStruct((z.table,), i32),
        in_specs=[SMEM] * 3,
        out_specs=SMEM,
        name="tables",
    )(me, lists, tile_count)


def split_kernel(z, k, me_ref, words_ref, *refs):
    outs, sem = refs[-1 - z.half : -1], refs[-1]
    place = lax.rem(me_ref[1], z.half)
    copies = []
    for s in range(z.half):
        row = pl.multiple_of((place ^ s) * z.part + k * z.step, 16)
        copies.append(pltpu.make_async_copy(words_ref.at[:, pl.ds(row, z.step)], outs[s], sem.at[s]))
    for copy in copies:
        copy.start()
    for copy in copies:
        copy.wait()


def split_words(z, k, me, words, after):
    return pl.pallas_call(
        functools.partial(split_kernel, z, k),
        out_shape=[jax.ShapeDtypeStruct((z.blocks, z.step, z.dim), bf16)] * z.half,
        in_specs=[SMEM, ANY] + [ANY] * len(after),
        out_specs=[VMEM] * z.half,
        scratch_shapes=[pltpu.SemaphoreType.DMA((z.half,))],
        name="split_words",
    )(me, words, *after)


def start_pick(sources, size, spot, target, sem):
    for s, source in enumerate(sources):
        @pl.when(jnp.logical_and(spot >= s * size, spot < (s + 1) * size))
        def _(s=s, source=source):
            pltpu.make_async_copy(source.at[spot - s * size], target, sem).start()


def lanes_kernel(z, cap, table_ref, *refs):
    pool, out_ref, sem = refs[: z.half], refs[-2], refs[-1]
    for j in range(cap):
        start_pick(pool, z.blocks, table_ref[z.at_send + j], out_ref.at[j], sem.at[j])
    for j in range(cap):
        pltpu.make_async_copy(pool[0].at[0], out_ref.at[j], sem.at[j]).wait()


def pick_lanes(z, cap, table, pool, after):
    return pl.pallas_call(
        functools.partial(lanes_kernel, z, cap),
        out_shape=jax.ShapeDtypeStruct((cap, z.step, z.dim), bf16),
        in_specs=[SMEM] + [ANY] * (z.half + len(after)),
        out_specs=VMEM,
        scratch_shapes=[pltpu.SemaphoreType.DMA((cap,))],
        name="pick_lanes",
    )(table, *pool, *after)


def asked_kernel(z, cap, table_ref, *refs):
    pool, lanes = refs[: z.half], refs[z.half]
    outs, sem = refs[-1 - z.half : -1], refs[-1]
    for s in range(z.half):
        for t in range(z.slots):
            n = s * z.slots + t
            spot = table_ref[z.at_fetch + n]
            start_pick(pool, z.blocks, spot, outs[s].at[t], sem.at[n])

            @pl.when(spot >= z.pool)
            def _():
                pltpu.make_async_copy(lanes.at[spot - z.pool], outs[s].at[t], sem.at[n]).start()

    for s in range(z.half):
        for t in range(z.slots):
            pltpu.make_async_copy(pool[0].at[0], outs[s].at[t], sem.at[s * z.slots + t]).wait()


def pick_asked(z, cap, table, pool, lanes, after):
    return pl.pallas_call(
        functools.partial(asked_kernel, z, cap),
        out_shape=[jax.ShapeDtypeStruct((z.slots, z.step, z.dim), bf16)] * z.half,
        in_specs=[SMEM] + [ANY] * (z.half + 1 + len(after)),
        out_specs=[VMEM] * z.half,
        scratch_shapes=[pltpu.SemaphoreType.DMA((z.half * z.slots,))],
        name="pick_asked",
    )(table, *pool, lanes, *after)


def tile_kernel(z, first, last, waits, info_ref, *refs):
    h = z.half
    refs = refs[waits:]
    words, refs = refs[:h], refs[h:]
    counts, refs = refs[:h], refs[h:]
    row_refs, refs = refs[:h], refs[h:]
    ctx_ref, col_ref, refs = refs[0], refs[1], refs[2:]
    if not first:
        so_far_ref, refs = refs[0], refs[1:]
    parts, refs = refs[:h], refs[h:]
    total_ref, w_ref, scores_ref, slope_ref = refs
    t = pl.program_id(0)
    n = z.step
    live = t < info_ref[0]

    @pl.when(jnp.logical_not(live))
    def _():
        total_ref[...] = jnp.zeros_like(total_ref)

    @pl.when(live)
    def _():
        c_tile = ctx_ref[0]
        col_term = jnp.log(col_ref[0].astype(f32)) - shift_term
        for s in range(h):
            w_ref[s * n : (s + 1) * n, :] = words[s][0]
        for s in range(h):
            rows = slice(s * n, (s + 1) * n)
            scores_ref[rows, :] = lax.dot_general(
                w_ref[rows, :], c_tile, (((1,), (1,)), ((), ())), preferred_element_type=f32
            )
            row_term = jnp.log(row_refs[s][0, 0].astype(f32))
            tall = jnp.transpose(jnp.broadcast_to(row_term, (128, n)))
            strip = 16
            for i in range(n // strip):
                at = s * n + i * strip
                occur = counts[s][0, i * strip : (i + 1) * strip, :].astype(f32)
                least = jnp.maximum(occur, 1.0)
                diff = scores_ref[at : at + strip, :] + col_term + tall[i * strip : (i + 1) * strip, :1]
                diff = diff - jnp.log(least)
                seen = (0.1 + 0.25 * (least * lax.rsqrt(least))) * diff
                unseen = 0.5 * jnp.tanh(0.5 * diff) + 0.5
                slope_ref[at : at + strip, :] = jnp.where(occur > 0, seen, unseen).astype(bf16)
        word_part = jnp.dot(slope_ref[...], c_tile, preferred_element_type=f32).astype(bf16)
        for s in range(h):
            parts[s][0] = word_part[s * n : (s + 1) * n]
        turned = lax.dot_general(
            w_ref[...], slope_ref[...], (((0,), (0,)), ((), ())), preferred_element_type=f32
        )
        if not first:
            turned = turned + so_far_ref[0]
        if last:
            total_ref[0] = jnp.transpose(turned).astype(bf16)
        else:
            total_ref[0] = turned


def tile_step(z, k, info, words, counts, row_sums, col_sums, ctx_tiles, so_far, after):
    first, last = so_far is None, k == chunks - 1
    h, n = z.half, z.step
    wide = (1, z.dim, z.block)
    tall = (1, z.block, z.dim)

    def counts_spec(s):
        return pl.BlockSpec((1, n, z.block), lambda t, info: (t, info[8 + s] * chunks + k, 0))

    def rows_spec(s):
        return pl.BlockSpec((1, 1, 1, n), lambda t, info: (t, info[8 + s] * chunks + k, 0, 0))

    word_spec = pl.BlockSpec((1, n, z.dim), lambda t, info: (t, 0, 0))
    by_owner = lambda t, info: (info[8 + h + t], 0, 0)
    by_slot = lambda t, info: (t, 0, 0)
    in_specs = [ANY] * len(after) + [word_spec] * h
    in_specs += [counts_spec(s) for s in range(h)]
    in_specs += [rows_spec(s) for s in range(h)]
    in_specs += [pl.BlockSpec(tall, by_owner), pl.BlockSpec((1, 1, z.block), by_slot)]
    args = [*after, *words, *([counts] * h), *([row_sums] * h), ctx_tiles, col_sums]
    if not first:
        in_specs.append(pl.BlockSpec(wide, by_slot))
        args.append(so_far)
    if last:
        total_shape = jax.ShapeDtypeStruct((z.slots, z.block, z.dim), bf16)
        total_spec = pl.BlockSpec(tall, by_owner)
    else:
        total_shape = jax.ShapeDtypeStruct((z.slots, z.dim, z.block), f32)
        total_spec = pl.BlockSpec(wide, by_slot)
    flops = 6 * z.slots * h * n * z.block * z.dim
    return pl.pallas_call(
        functools.partial(tile_kernel, z, first, last, len(after)),
        out_shape=[jax.ShapeDtypeStruct((z.slots, n, z.dim), bf16)] * h + [total_shape],
        grid_spec=pltpu.PrefetchScalarGridSpec(
            num_scalar_prefetch=1,
            grid=(z.slots,),
            in_specs=in_specs,
            out_specs=[word_spec] * h + [total_spec],
            scratch_shapes=[
                pltpu.VMEM((h * n, z.dim), bf16),
                pltpu.VMEM((h * n, z.block), f32),
                pltpu.VMEM((h * n, z.block), bf16),
            ],
        ),
        compiler_params=big,
        name="tile_step",
    )(info, *args)


def gather_kernel(z, cap, table_ref, *refs):
    h = z.half
    parts, (own_ref, lanes_ref, total) = refs[:h], refs[-3:]
    total[...] = jnp.zeros_like(total)
    for s in range(h):
        for t in range(z.slots):
            n = s * z.slots + t
            @pl.when(table_ref[z.at_live + n] != 0)
            def _(s=s, t=t, n=n):
                spot = table_ref[z.at_fetch + n]
                total[spot] = total[spot] + parts[s][t].astype(f32)
    own_ref[...] = total[: z.pool]
    lanes_ref[...] = total[z.pool :].astype(bf16)


def sum_parts(z, cap, table, parts, after):
    n = z.step
    return pl.pallas_call(
        functools.partial(gather_kernel, z, cap),
        out_shape=[
            jax.ShapeDtypeStruct((z.pool, n, z.dim), f32),
            jax.ShapeDtypeStruct((cap, n, z.dim), bf16),
        ],
        in_specs=[SMEM] + [VMEM] * z.half + [ANY] * len(after),
        out_specs=[VMEM, VMEM],
        scratch_shapes=[pltpu.VMEM((z.pool + cap, n, z.dim), f32)],
        compiler_params=big,
        name="sum_parts",
    )(table, *parts, *after)


def word_kernel(z, table_ref, own_ref, lanes_ref, *refs):
    pool, outs = refs[: z.half], refs[z.half :]
    for p in range(z.pool):
        s, b = p // z.blocks, p % z.blocks
        rank = table_ref[z.at_rank + p]
        extra = lanes_ref[jnp.maximum(rank, 0)].astype(f32)
        grad = own_ref[p] + jnp.where(rank >= 0, extra, jnp.zeros_like(extra))
        outs[s][b] = (pool[s][b].astype(f32) - learn_rate * grad).astype(bf16)


def word_step(z, table, own, lanes, pool):
    return pl.pallas_call(
        functools.partial(word_kernel, z),
        out_shape=[jax.ShapeDtypeStruct((z.blocks, z.step, z.dim), bf16)] * z.half,
        in_specs=[SMEM] + [VMEM] * (2 + z.half),
        out_specs=[VMEM] * z.half,
        compiler_params=big,
        name="word_step",
    )(table, own, lanes, *pool)


def join_kernel(z, me_ref, *refs):
    pieces, out_ref, sem = refs[:-2], refs[-2], refs[-1]
    place = lax.rem(me_ref[1], z.half)
    copies = []
    for n, piece in enumerate(pieces):
        k, s = n // z.half, n % z.half
        row = pl.multiple_of((place ^ s) * z.part + k * z.step, 16)
        copies.append(pltpu.make_async_copy(piece, out_ref.at[:, pl.ds(row, z.step)], sem.at[n]))
    for copy in copies:
        copy.start()
    for copy in copies:
        copy.wait()


def join_words(z, me, pieces):
    return pl.pallas_call(
        functools.partial(join_kernel, z),
        out_shape=jax.ShapeDtypeStruct((z.blocks, z.block, z.dim), bf16),
        in_specs=[SMEM] + [ANY] * len(pieces),
        out_specs=VMEM,
        scratch_shapes=[pltpu.SemaphoreType.DMA((len(pieces),))],
        name="join_words",
    )(me, *pieces)


def give_kernel(z, info_ref, ctx_ref, *refs):
    out_ref, sem = refs[-2:]
    copies = []
    for p in range(z.rows):
        b = info_ref[8 + z.half + z.slots + p]
        copies.append(pltpu.make_async_copy(ctx_ref.at[b], out_ref.at[p], sem.at[p]))
    for copy in copies:
        copy.start()
    for copy in copies:
        copy.wait()


def give_contexts(z, info, contexts, after):
    return pl.pallas_call(
        functools.partial(give_kernel, z),
        out_shape=jax.ShapeDtypeStruct((z.rows, z.block, z.dim), bf16),
        in_specs=[SMEM, ANY] + [ANY] * len(after),
        out_specs=VMEM,
        scratch_shapes=[pltpu.SemaphoreType.DMA((z.rows,))],
        name="give_contexts",
    )(info, contexts, *after)


def context_kernel(z, info_ref, back_ref, ctx_ref, out_ref, total):
    total[...] = jnp.zeros_like(total)
    for p in range(z.rows):
        b = info_ref[8 + z.half + z.slots + p]
        total[b] = total[b] + back_ref[p].astype(f32)
    out_ref[...] = (ctx_ref[...].astype(f32) - learn_rate * total[...]).astype(bf16)


def context_step(z, info, back, contexts):
    n = z.block // 4
    return pl.pallas_call(
        functools.partial(context_kernel, z),
        out_shape=jax.ShapeDtypeStruct((z.blocks, z.block, z.dim), bf16),
        grid_spec=pltpu.PrefetchScalarGridSpec(
            num_scalar_prefetch=1,
            grid=(4,),
            in_specs=[
                pl.BlockSpec((z.rows, n, z.dim), lambda i, info: (0, i, 0)),
                pl.BlockSpec((z.blocks, n, z.dim), lambda i, info: (0, i, 0)),
            ],
            out_specs=pl.BlockSpec((z.blocks, n, z.dim), lambda i, info: (0, i, 0)),
            scratch_shapes=[pltpu.VMEM((z.blocks, n, z.dim), f32)],
        ),
        compiler_params=big,
        name="context_step",
    )(info, back, contexts)


def local(word_vecs, ctx_vecs, tile_rows, tile_cols, tile_count, counts, row_sums, col_sums):
    z = Sizes(word_vecs, counts)
    own_row, own_col = lax.axis_index("row"), lax.axis_index("col")
    place = own_col % z.half
    words = word_vecs[:, 0]
    contexts = ctx_vecs[:, 0]
    counts = counts[0, 0]
    row_sums = row_sums[0, 0].reshape(z.slots, z.half * chunks, 1, z.step)
    col_sums = col_sums[0, 0].reshape(z.slots, 1, z.block)
    me = jnp.stack([own_row, own_col]).astype(i32)

    def spread(k, after):
        pieces = split_words(z, k, me, words, after)
        return [pieces[0]] + [swap(pieces[s], "col", s) for s in range(1, z.half)]

    flat = tile_rows.reshape(1, z.cols * z.slots)
    lists = jnp.concatenate([flat] + [swap(flat, "row", s) for s in range(1, z.rows)])
    pool_0 = spread(0, [])
    table = make_table(z, me, lists, tile_count)

    col_lists = tile_cols[:, 0]
    mine = lax.dynamic_index_in_dim(col_lists, own_row, 0, False)
    live = tile_count[own_row, own_col]
    given = jnp.sum(jnp.where(col_lists // z.blocks == own_row, col_lists % z.blocks, 0), axis=1)
    info = jnp.concatenate(
        [
            jnp.full((8,), live, i32),
            place ^ jnp.arange(z.half, dtype=i32),
            mine // z.blocks,
            given,
        ]
    ).astype(i32)

    def exchange(pieces):
        return [pieces[0]] + [swap(pieces[s], "col", s) for s in range(1, z.half)]

    def rest(cap):
        def run(pool_0, table):
            outgoing = give_contexts(z, info, contexts, [])
            ctx_tiles = lax.all_to_all(outgoing, "row", 0, 0, tiled=True)
            pools = [list(pool_0)] + [spread(k, []) for k in range(1, chunks)]
            so_far, lanes, asked, made, own, returned, pieces = None, [], [], [], [], [], []
            for k in range(chunks):
                lanes.append(across_col(pick_lanes(z, cap, table, pools[k], lanes[-1:])))
                order = []
                asked.append(pick_asked(z, cap, table, pools[k], lanes[k], order))
                *out, so_far = tile_step(
                    z, k, info, exchange(asked[k]), counts, row_sums, col_sums, ctx_tiles, so_far, []
                )
                made.append(out)
            for k in range(chunks):
                order = returned[-1:]
                sum_step(k, cap, table, exchange(made[k]), own, returned, order)
                pieces += exchange(word_step(z, table, own[k], returned[k], pools[k]))
            back = lax.all_to_all(so_far, "row", 0, 0, tiled=True)
            new_contexts = context_step(z, info, back, contexts)
            return join_words(z, me, pieces), new_contexts

        def sum_step(k, cap, table, parts, own, returned, after):
            total, grads = sum_parts(z, cap, table, parts, after)
            own.append(total)
            returned.append(across_col(grads))
            return [grads]

        return run

    def across_col(x):
        return swap(x, "col", z.half)

    caps = sorted({max(1, z.pool * n // 16) for n in (9, 16)})
    level = sum((table[0] > cap).astype(i32) for cap in caps[:-1])
    new_words, new_contexts = lax.switch(level, [rest(cap) for cap in caps], tuple(pool_0), table)
    return new_words[:, None], new_contexts[:, None]


def solution(mesh):
    placed = (
        P("col", "row", None, None),
        P("row", "col", None, None),
        P("row", None, None),
        P(None, "col", None),
        P(),
        P("row", "col", None, None, None),
        P("row", "col", None, None),
        P("row", "col", None, None),
    )
    return jax.shard_map(
        local,
        mesh=mesh,
        in_specs=placed,
        out_specs=(P("col", "row", None, None), P("row", "col", None, None)),
        check_vma=False,
    )
```

profile of v0, /device:TPU:0, one launch (start us, length us, event | category | flops | bytes accessed | tf_op | source)
XLA Modules:
  0.0 214.4 jit_solution(12871759471415192268)
XLA Ops:
  0.7 0.9 copy.17
  1.7 2.4 %collective-permute-start.52 = (s32[1,32]{1,0:T(1,128)S(1)}, s32[1,32]{1,0:T(1,128)S(1)}, u32[]{:S(2)}, u32[]{:S(2)}) collective-permute-start(s32[1,32]{1,0:T(1,128)S(1)} %reshape.15), channel_id=1, source_target_pairs={{0,24},{8,16},{16,8},{24,0},{1,25},{9,17},{17,9},{25,1},{2,26},{10... | collective-permute-start | bytes 392 | tf_op jit(solution)/shard_map/ppermute | solution.py:22
  4.0 0.6 collective-permute-start.51
  4.8 2.6 %split_words.5 = (bf16[4,128,256]{2,1,0:T(8,128)(2,1)S(1)}, bf16[4,128,256]{2,1,0:T(8,128)(2,1)}, bf16[4,128,256]{2,1,0:T(8,128)(2,1)}, bf16[4,128,256]{2,1,0:T(8,128)(2,1)}) custom-call(s32[2]{0:T(128)S(1)} %pad_add_fusion.1.me_ref, bf16[4,1024,256]{2,1,0:T(8,128)(2,1)} %bitcast.33), custom_call_target="tpu_custom_call" | custom-call | tf_op jit(solution)/shard_map/split_words/pallas_call | solution.py:146
  7.4 1.6 collective-permute-start.53
  9.0 1.6 collective-permute-start.54
  11.1 1.3 dynamic_slice.7
  13.2 1.1 collective-permute-done.50
  14.3 0.6 pad_add_fusion.lists_ref
  14.8 2.8 %tables.1 = s32[72]{0:T(128)S(1)} custom-call(s32[2]{0:T(128)S(1)} %pad_add_fusion.1.me_ref, s32[4,32]{1,0:T(4,128)} %pad_add_fusion.lists_ref, s32[4,8]{1,0:T(4,128)} %count_ref.1), custom_call_target="tpu_custom_call" | custom-call | tf_op jit(solution)/shard_map/tables/pallas_call | solution.py:123
  17.7 0.7 collective-permute-done.54
  18.4 4.5 %collective-permute-done.55 = bf16[4,128,256]{2,1,0:T(8,128)(2,1)S(1)} collective-permute-done((bf16[4,128,256]{2,1,0:T(8,128)(2,1)}, bf16[4,128,256]{2,1,0:T(8,128)(2,1)S(1)}, u32[]{:S(2)}, u32[]{:S(2)}) %collective-permute-start.55) | collective-permute-done | bytes 262176 | tf_op jit(solution)/shard_map/ppermute | solution.py:22
  22.8 191.4 %conditional.1 = (bf16[4,1,1024,256]{3,2,1,0:T(8,128)(2,1)}, bf16[4,1,1024,256]{3,2,1,0:T(8,128)(2,1)}) conditional(s32[]{:T(128)} %bitcast.14, (s32[72]{0:T(128)S(1)}, bf16[4,128,256]{2,1,0:T(8,128)(2,1)S(1)}, bf16[4,128,256]{2,1,0:T(8,128)(2,1)S(1)}, bf16[4,128,256]{2,1,0:T(8,128)(2,1)S(1)}, bf16[4,128,256]{2,1,0:T(8,128)(2,1)S(1)}, ...), branch_computations={%region_1.2_spmd, %region_2.3_spmd} | conditional | bytes 138413840 | solution.py:515
  22.9 2.4 %give_contexts.2 = bf16[4,1024,256]{2,1,0:T(8,128)(2,1)} custom-call(s32[20]{0:T(128)S(1)} %get-tuple-element.52.info_ref, bf16[4,1024,256]{2,1,0:T(8,128)(2,1)S(1)} %get-tuple-element.63.ctx_ref), custom_call_target="tpu_custom_call" | custom-call | tf_op jit(solution)/shard_map/cond/branch_0_fun/give_contexts/pallas_call | solution.py:406
  25.2 3.6 %all-to-all-start = ((bf16[4,1024,256]{2,1,0:T(8,128)(2,1)}), bf16[4,1024,256]{2,1,0:T(8,128)(2,1)S(1)}, u32[]{:S(2)}, u32[]{:S(2)}) async-start(bf16[4,1024,256]{2,1,0:T(8,128)(2,1)} %give_contexts.2), calls=%async_computation | async-start | bytes 4194304 | tf_op jit(solution)/shard_map/cond/branch_0_fun/all_to_all | solution.py:483
  28.9 2.4 %pick_lanes.4 = bf16[9,128,256]{2,1,0:T(8,128)(2,1)} custom-call(s32[72]{0:T(128)S(1)} %get-tuple-element.51.table_ref, bf16[4,128,256]{2,1,0:T(8,128)(2,1)S(1)} %get-tuple-element.53.refs_0_, bf16[4,128,256]{2,1,0:T(8,128)(2,1)S(1)} %get-tuple-element.54.refs_1_, bf16[4,128,256]{2,1,0:T(8,128)(2,1)S(1)} %get-tuple-element.55.refs_2_, ...), custom_call_target="tpu_custom_call" | custom-call | tf_op jit(solution)/shard_map/cond/branch_0_fun/pick_lanes/pallas_call | solution.py:172
  31.3 2.8 %collective-permute-start = (bf16[9,128,256]{2,1,0:T(8,128)(2,1)}, bf16[9,128,256]{2,1,0:T(8,128)(2,1)}, u32[]{:S(2)}, u32[]{:S(2)}) collective-permute-start(bf16[9,128,256]{2,1,0:T(8,128)(2,1)} %pick_lanes.4), channel_id=1, source_target_pairs={{0,4},{1,5},{2,6},{3,7},{4,0},{5,1},{6,2},{7,3},{8,12},{9,13},{10,... | collective-permute-start | bytes 1769480 | tf_op jit(solution)/shard_map/cond/branch_0_fun/ppermute | solution.py:22
  34.1 2.8 %split_words.3 = (bf16[4,128,256]{2,1,0:T(8,128)(2,1)}, bf16[4,128,256]{2,1,0:T(8,128)(2,1)}, bf16[4,128,256]{2,1,0:T(8,128)(2,1)}, bf16[4,128,256]{2,1,0:T(8,128)(2,1)}) custom-call(s32[2]{0:T(128)S(1)} %get-tuple-element.50.me_ref, bf16[4,1024,256]{2,1,0:T(8,128)(2,1)} %get-tuple-element.75.words_ref), custom_call_target="tpu_custom_call" | custom-call | tf_op jit(solution)/shard_map/cond/branch_0_fun/split_words/pallas_call | solution.py:146
  36.9 1.6 collective-permute-start.11
  38.5 1.6 collective-permute-start.12
  40.5 5.1 %collective-permute-done.11.refs_1_ = bf16[4,128,256]{2,1,0:T(8,128)(2,1)S(1)} collective-permute-done((bf16[4,128,256]{2,1,0:T(8,128)(2,1)}, bf16[4,128,256]{2,1,0:T(8,128)(2,1)S(1)}, u32[]{:S(2)}, u32[]{:S(2)}) %collective-permute-start.11) | collective-permute-done | bytes 262176 | tf_op jit(solution)/shard_map/cond/branch_0_fun/ppermute | solution.py:22
  45.6 8.2 %collective-permute-done.12.refs_2_ = bf16[4,128,256]{2,1,0:T(8,128)(2,1)S(1)} collective-permute-done((bf16[4,128,256]{2,1,0:T(8,128)(2,1)}, bf16[4,128,256]{2,1,0:T(8,128)(2,1)S(1)}, u32[]{:S(2)}, u32[]{:S(2)}) %collective-permute-start.12) | collective-permute-done | bytes 262176 | tf_op jit(solution)/shard_map/cond/branch_0_fun/ppermute | solution.py:22
  53.8 10.1 %collective-permute-done.13.refs_3_ = bf16[4,128,256]{2,1,0:T(8,128)(2,1)S(1)} collective-permute-done((bf16[4,128,256]{2,1,0:T(8,128)(2,1)}, bf16[4,128,256]{2,1,0:T(8,128)(2,1)S(1)}, u32[]{:S(2)}, u32[]{:S(2)}) %collective-permute-start.13) | collective-permute-done | bytes 262176 | tf_op jit(solution)/shard_map/cond/branch_0_fun/ppermute | solution.py:22
  63.9 0.7 copy-done.7
  64.6 2.5 %pick_lanes.5 = bf16[9,128,256]{2,1,0:T(8,128)(2,1)} custom-call(s32[72]{0:T(128)S(1)} %get-tuple-element.51.table_ref, bf16[4,128,256]{2,1,0:T(8,128)(2,1)} %get-tuple-element.76.refs_0_, bf16[4,128,256]{2,1,0:T(8,128)(2,1)} %copy-done.3, bf16[4,128,256]{2,1,0:T(8,128)(2,1)} %copy-done.5, bf16[4,128,256]{2,1,0:T(8,128)(2,1)} %copy-done.7, ...), custom_call_target="tpu_custom_call" | custom-call | tf_op jit(solution)/shard_map/cond/branch_0_fun/pick_lanes/pallas_call | solution.py:172
  67.1 0.8 collective-permute-start.14
  67.9 3.3 %pick_asked.4 = (bf16[4,128,256]{2,1,0:T(8,128)(2,1)}, bf16[4,128,256]{2,1,0:T(8,128)(2,1)}, bf16[4,128,256]{2,1,0:T(8,128)(2,1)}, bf16[4,128,256]{2,1,0:T(8,128)(2,1)}) custom-call(s32[72]{0:T(128)S(1)} %get-tuple-element.51.table_ref, bf16[4,128,256]{2,1,0:T(8,128)(2,1)S(1)} %get-tuple-element.53.refs_0_, ...), custom_call_target="tpu_custom_call" | custom-call | tf_op jit(solution)/shard_map/cond/branch_0_fun/pick_asked/pallas_call | solution.py:201
  71.2 0.9 collective-permute-start.1
  72.1 3.2 %collective-permute-start.2 = (bf16[4,128,256]{2,1,0:T(8,128)(2,1)}, bf16[4,128,256]{2,1,0:T(8,128)(2,1)S(1)}, u32[]{:S(2)}, u32[]{:S(2)}) collective-permute-start(bf16[4,128,256]{2,1,0:T(8,128)(2,1)} %get-tuple-element.59), channel_id=1, source_target_pairs={{0,2},{1,3},{2,0},{3,1},{4,6},{5,7},{6,4},{7,5},{8,10},{9,11},{10,... | collective-permute-start | bytes 786440 | tf_op jit(solution)/shard_map/cond/branch_0_fun/ppermute | solution.py:22
  75.2 19.3 %collective-permute-done.14.refs_4_ = bf16[9,128,256]{2,1,0:T(8,128)(2,1)} collective-permute-done((bf16[9,128,256]{2,1,0:T(8,128)(2,1)}, bf16[9,128,256]{2,1,0:T(8,128)(2,1)}, u32[]{:S(2)}, u32[]{:S(2)}) %collective-permute-start.14) | collective-permute-done | bytes 589856 | tf_op jit(solution)/shard_map/cond/branch_0_fun/ppermute | solution.py:22
  94.6 2.9 %pick_asked.5 = (bf16[4,128,256]{2,1,0:T(8,128)(2,1)}, bf16[4,128,256]{2,1,0:T(8,128)(2,1)}, bf16[4,128,256]{2,1,0:T(8,128)(2,1)}, bf16[4,128,256]{2,1,0:T(8,128)(2,1)}) custom-call(s32[72]{0:T(128)S(1)} %get-tuple-element.51.table_ref, bf16[4,128,256]{2,1,0:T(8,128)(2,1)} %get-tuple-element.76.refs_0_, bf16[4,128,256]{2,1,0:T(8,128)(2,1)} %copy-done.3, ...), custom_call_target="tpu_custom_call" | custom-call | tf_op jit(solution)/shard_map/cond/branch_0_fun/pick_asked/pallas_call | solution.py:201
  97.5 2.2 %collective-permute-start.15 = (bf16[4,128,256]{2,1,0:T(8,128)(2,1)}, bf16[4,128,256]{2,1,0:T(8,128)(2,1)S(1)}, u32[]{:S(2)}, u32[]{:S(2)}) collective-permute-start(bf16[4,128,256]{2,1,0:T(8,128)(2,1)} %get-tuple-element.81), channel_id=1, source_target_pairs={{0,1},{1,0},{2,3},{3,2},{4,5},{5,4},{6,7},{7,6},{8,9},{9,8},{10,11... | collective-permute-start | bytes 786440 | tf_op jit(solution)/shard_map/cond/branch_0_fun/ppermute | solution.py:22
  99.7 1.5 collective-permute-start.17
  101.2 0.9 copy-done.21
  102.2 10.5 %tile_step.4 = (bf16[4,128,256]{2,1,0:T(8,128)(2,1)S(1)}, bf16[4,128,256]{2,1,0:T(8,128)(2,1)}, bf16[4,128,256]{2,1,0:T(8,128)(2,1)}, bf16[4,128,256]{2,1,0:T(8,128)(2,1)}, f32[4,256,1024]{2,1,0:T(8,128)S(1)}) custom-call(s32[20]{0:T(128)S(1)} %get-tuple-element.52.info_ref, bf16[4,128,256]{2,1,0:T(8,128)(2,1)S(1)} %copy-done.21, ...), custom_call_target="tpu_custom_call" | custom-call | tf_op jit(solution)/shard_map/cond/branch_0_fun/tile_step/pallas_call | solution.py:297
  112.7 0.7 copy-done.28
  113.5 3.4 %collective-permute-start.6 = (bf16[4,128,256]{2,1,0:T(8,128)(2,1)}, bf16[4,128,256]{2,1,0:T(8,128)(2,1)}, u32[]{:S(2)}, u32[]{:S(2)}) collective-permute-start(bf16[4,128,256]{2,1,0:T(8,128)(2,1)} %get-tuple-element.68), channel_id=1, source_target_pairs={{0,3},{1,2},{2,1},{3,0},{4,7},{5,6},{6,5},{7,4},{8,11},{9,10},{10,... | collective-permute-start | bytes 786440 | tf_op jit(solution)/shard_map/cond/branch_0_fun/ppermute | solution.py:22
  116.9 10.2 %tile_step.5 = (bf16[4,128,256]{2,1,0:T(8,128)(2,1)S(1)}, bf16[4,128,256]{2,1,0:T(8,128)(2,1)S(1)}, bf16[4,128,256]{2,1,0:T(8,128)(2,1)S(1)}, bf16[4,128,256]{2,1,0:T(8,128)(2,1)S(1)}, bf16[4,1024,256]{2,1,0:T(8,128)(2,1)S(1)}) custom-call(s32[20]{0:T(128)S(1)} %get-tuple-element.52.info_ref, bf16[4,128,256]{2,1,0:T(8,128)(2,1)S(1)} %copy-done.20, ...), custom_call_target="tpu_custom_call" | custom-call | tf_op jit(solution)/shard_map/cond/branch_0_fun/tile_step/pallas_call | solution.py:297
  127.1 1.3 copy-done.16
  128.4 0.7 copy-done.30
  129.1 0.7 copy-done.32
  129.8 0.7 copy-done.34
  130.5 3.7 %all-to-all-start.1 = ((bf16[4,1024,256]{2,1,0:T(8,128)(2,1)}), bf16[4,1024,256]{2,1,0:T(8,128)(2,1)S(1)}, u32[]{:S(2)}, u32[]{:S(2)}) async-start(bf16[4,1024,256]{2,1,0:T(8,128)(2,1)} %copy-done.16), calls=%async_computation.1 | async-start | bytes 4194304 | tf_op jit(solution)/shard_map/cond/branch_0_fun/all_to_all | solution.py:498
  134.3 1.8 sum_parts.4
  137.7 2.5 %collective-permute-start.20 = (bf16[4,128,256]{2,1,0:T(8,128)(2,1)S(1)}, bf16[4,128,256]{2,1,0:T(8,128)(2,1)S(1)}, u32[]{:S(2)}, u32[]{:S(2)}) collective-permute-start(bf16[4,128,256]{2,1,0:T(8,128)(2,1)S(1)} %copy-done.31), channel_id=1, source_target_pairs={{0,3},{1,2},{2,1},{3,0},{4,7},{5,6},{6,5},{7,4},{8,11},{9,10},{10,... | collective-permute-start | bytes 786440 | tf_op jit(solution)/shard_map/cond/branch_0_fun/ppermute | solution.py:22
  140.2 5.1 %collective-permute-done.18.refs_1_ = bf16[4,128,256]{2,1,0:T(8,128)(2,1)S(1)} collective-permute-done((bf16[4,128,256]{2,1,0:T(8,128)(2,1)}, bf16[4,128,256]{2,1,0:T(8,128)(2,1)S(1)}, u32[]{:S(2)}, u32[]{:S(2)}) %collective-permute-start.18) | collective-permute-done | bytes 262176 | tf_op jit(solution)/shard_map/cond/branch_0_fun/ppermute | solution.py:22
  145.3 10.7 %collective-permute-done.19.refs_2_ = bf16[4,128,256]{2,1,0:T(8,128)(2,1)S(1)} collective-permute-done((bf16[4,128,256]{2,1,0:T(8,128)(2,1)S(1)}, bf16[4,128,256]{2,1,0:T(8,128)(2,1)S(1)}, u32[]{:S(2)}, u32[]{:S(2)}) %collective-permute-start.19) | collective-permute-done | bytes 262176 | tf_op jit(solution)/shard_map/cond/branch_0_fun/ppermute | solution.py:22
  156.0 5.2 %collective-permute-done.20.refs_3_ = bf16[4,128,256]{2,1,0:T(8,128)(2,1)S(1)} collective-permute-done((bf16[4,128,256]{2,1,0:T(8,128)(2,1)S(1)}, bf16[4,128,256]{2,1,0:T(8,128)(2,1)S(1)}, u32[]{:S(2)}, u32[]{:S(2)}) %collective-permute-start.20) | collective-permute-done | bytes 262176 | tf_op jit(solution)/shard_map/cond/branch_0_fun/ppermute | solution.py:22
  161.2 3.2 %collective-permute-done.7.lanes_ref.refs_4_ = bf16[9,128,256]{2,1,0:T(8,128)(2,1)S(1)} collective-permute-done((bf16[9,128,256]{2,1,0:T(8,128)(2,1)S(1)}, bf16[9,128,256]{2,1,0:T(8,128)(2,1)S(1)}, u32[]{:S(2)}, u32[]{:S(2)}) %collective-permute-start.7) | collective-permute-done | bytes 589856 | tf_op jit(solution)/shard_map/cond/branch_0_fun/ppermute | solution.py:22
  164.4 1.2 sum_parts.5
  165.8 1.0 word_step.4
  166.8 1.5 collective-permute-start.8
  168.3 1.1 collective-permute-start.9
  169.4 1.4 collective-permute-start.10
  170.8 22.9 %collective-permute-done.21.lanes_ref = bf16[9,128,256]{2,1,0:T(8,128)(2,1)S(1)} collective-permute-done((bf16[9,128,256]{2,1,0:T(8,128)(2,1)S(1)}, bf16[9,128,256]{2,1,0:T(8,128)(2,1)S(1)}, u32[]{:S(2)}, u32[]{:S(2)}) %collective-permute-start.21) | collective-permute-done | bytes 589856 | tf_op jit(solution)/shard_map/cond/branch_0_fun/ppermute | solution.py:22
  193.7 1.0 word_step.5
  194.7 0.7 copy-done.26
  195.4 0.8 collective-permute-start.22
  196.2 0.7 copy-done.52
  196.9 2.7 %collective-permute-start.24 = (bf16[4,128,256]{2,1,0:T(8,128)(2,1)S(1)}, bf16[4,128,256]{2,1,0:T(8,128)(2,1)}, u32[]{:S(2)}, u32[]{:S(2)}) collective-permute-start(bf16[4,128,256]{2,1,0:T(8,128)(2,1)S(1)} %get-tuple-element.94), channel_id=1, source_target_pairs={{0,3},{1,2},{2,1},{3,0},{4,7},{5,6},{6,5},{7,4},{8,11},{9,10},{10,... | collective-permute-start | bytes 786440 | tf_op jit(solution)/shard_map/cond/branch_0_fun/ppermute | solution.py:22
  199.6 5.1 %context_step.2 = bf16[4,1024,256]{2,1,0:T(8,128)(2,1)} custom-call(s32[20]{0:T(128)S(1)} %get-tuple-element.52.info_ref, bf16[4,1024,256]{2,1,0:T(8,128)(2,1)S(1)} %all-to-all-done.1.back_ref, bf16[4,1024,256]{2,1,0:T(8,128)(2,1)} %copy-done.36), custom_call_target="tpu_custom_call" | custom-call | tf_op jit(solution)/shard_map/cond/branch_0_fun/context_step/pallas_call | solution.py:426
  204.7 0.8 collective-permute-done.23.refs_6_
  205.5 5.1 %collective-permute-done.24.refs_7_ = bf16[4,128,256]{2,1,0:T(8,128)(2,1)} collective-permute-done((bf16[4,128,256]{2,1,0:T(8,128)(2,1)S(1)}, bf16[4,128,256]{2,1,0:T(8,128)(2,1)}, u32[]{:S(2)}, u32[]{:S(2)}) %collective-permute-start.24) | collective-permute-done | bytes 262176 | tf_op jit(solution)/shard_map/cond/branch_0_fun/ppermute | solution.py:22
  210.6 3.4 %join_words.2 = bf16[4,1024,256]{2,1,0:T(8,128)(2,1)} custom-call(s32[2]{0:T(128)S(1)} %get-tuple-element.50.me_ref, bf16[4,128,256]{2,1,0:T(8,128)(2,1)} %copy-done.24, bf16[4,128,256]{2,1,0:T(8,128)(2,1)} %copy-done.52, bf16[4,128,256]{2,1,0:T(8,128)(2,1)} %collective-permute-done.9.refs_2_, bf16[4,128,256]{2,1,0:T(8,128)(2,1)} %collective-permute-done.10.refs_3_, ...), custom_call_target="tpu_custom_call" | custom-call | tf_op jit(solution)/shard_map/cond/branch_0_fun/join_words/pallas_call | solution.py:383
  (96 shorter events, 3.8 us)
Async XLA Ops:
  0.6 10.3 %copy-start.57 = (s32[4,1,4]{2,1,0:T(1,128)S(1)}, s32[4,1,4]{2,1,0:T(1,128)}, u32[]{:S(2)}) copy-start(s32[4,1,4]{2,1,0:T(1,128)} %param.13) | copy-start | bytes 196
  0.6 12.4 %copy-start.55 = (s32[1,1,4,1024]{3,2,1,0:T(4,128)S(1)}, s32[1,1,4,1024]{3,2,1,0:T(4,128)}, u32[]{:S(2)}) copy-start(s32[1,1,4,1024]{3,2,1,0:T(4,128)} %param.16) | copy-start | bytes 49156
  0.7 12.5 %copy-start.56 = (s32[1,1,4,1024]{3,2,1,0:T(4,128)S(1)}, s32[1,1,4,1024]{3,2,1,0:T(4,128)}, u32[]{:S(2)}) copy-start(s32[1,1,4,1024]{3,2,1,0:T(4,128)} %param.17) | copy-start | bytes 49156
  0.7 22.2 %copy-start.35 = (bf16[4,1,1024,256]{3,2,1,0:T(8,128)(2,1)S(1)}, bf16[4,1,1024,256]{3,2,1,0:T(8,128)(2,1)}, u32[]{:S(2)}) copy-start(bf16[4,1,1024,256]{3,2,1,0:T(8,128)(2,1)} %param.11) | copy-start | bytes 6291460
  1.7 11.4 %collective-permute-start.52 = (s32[1,32]{1,0:T(1,128)S(1)}, s32[1,32]{1,0:T(1,128)S(1)}, u32[]{:S(2)}, u32[]{:S(2)}) collective-permute-start(s32[1,32]{1,0:T(1,128)S(1)} %reshape.15), channel_id=1, source_target_pairs={{0,24},{8,16},{16,8},{24,0},{1,25},{9,17},{17,9},{25,1},{2,26},{10... | collective-permute-start | bytes 392 | tf_op jit(solution)/shard_map/ppermute | solution.py:22
  4.0 9.1 %collective-permute-start.51 = (s32[1,32]{1,0:T(1,128)S(1)}, s32[1,32]{1,0:T(1,128)S(1)}, u32[]{:S(2)}, u32[]{:S(2)}) collective-permute-start(s32[1,32]{1,0:T(1,128)S(1)} %reshape.15), channel_id=1, source_target_pairs={{0,16},{8,24},{16,0},{24,8},{1,17},{9,25},{17,1},{25,9},{2,18},{10... | collective-permute-start | bytes 392 | tf_op jit(solution)/shard_map/ppermute | solution.py:22
  7.4 10.3 %collective-permute-start.53 = (bf16[4,128,256]{2,1,0:T(8,128)(2,1)}, bf16[4,128,256]{2,1,0:T(8,128)(2,1)S(1)}, u32[]{:S(2)}, u32[]{:S(2)}) collective-permute-start(bf16[4,128,256]{2,1,0:T(8,128)(2,1)} %get-tuple-element.149), channel_id=1, source_target_pairs={{0,1},{1,0},{2,3},{3,2},{4,5},{5,4},{6,7},{7,6},{8,9},{9,8},{10,11... | collective-permute-start | bytes 786440 | tf_op jit(solution)/shard_map/ppermute | solution.py:22
  9.0 9.4 %collective-permute-start.54 = (bf16[4,128,256]{2,1,0:T(8,128)(2,1)}, bf16[4,128,256]{2,1,0:T(8,128)(2,1)S(1)}, u32[]{:S(2)}, u32[]{:S(2)}) collective-permute-start(bf16[4,128,256]{2,1,0:T(8,128)(2,1)} %get-tuple-element.150), channel_id=1, source_target_pairs={{0,2},{1,3},{2,0},{3,1},{4,6},{5,7},{6,4},{7,5},{8,10},{9,11},{10,... | collective-permute-start | bytes 786440 | tf_op jit(solution)/shard_map/ppermute | solution.py:22
  10.6 12.3 %collective-permute-start.55 = (bf16[4,128,256]{2,1,0:T(8,128)(2,1)}, bf16[4,128,256]{2,1,0:T(8,128)(2,1)S(1)}, u32[]{:S(2)}, u32[]{:S(2)}) collective-permute-start(bf16[4,128,256]{2,1,0:T(8,128)(2,1)} %get-tuple-element.151), channel_id=1, source_target_pairs={{0,3},{1,2},{2,1},{3,0},{4,7},{5,6},{6,5},{7,4},{8,11},{9,10},{10,... | collective-permute-start | bytes 786440 | tf_op jit(solution)/shard_map/ppermute | solution.py:22
  13.1 1.2 collective-permute-start.50
  22.8 2.4 %copy-start.36 = (bf16[4,1024,256]{2,1,0:T(8,128)(2,1)}, bf16[4,1024,256]{2,1,0:T(8,128)(2,1)S(1)}, u32[]{:S(2)}) copy-start(bf16[4,1024,256]{2,1,0:T(8,128)(2,1)S(1)} %get-tuple-element.63.ctx_ref) | copy-start | bytes 6291460 | tf_op jit(solution)/shard_map/cond
  22.8 6.0 %copy-start.46 = (bf16[4,128,256]{2,1,0:T(8,128)(2,1)}, bf16[4,128,256]{2,1,0:T(8,128)(2,1)S(1)}, u32[]{:S(2)}) copy-start(bf16[4,128,256]{2,1,0:T(8,128)(2,1)S(1)} %get-tuple-element.55.refs_2_) | copy-start | bytes 786436 | tf_op jit(solution)/shard_map/cond
  22.8 6.0 %copy-start.49 = (bf16[4,128,256]{2,1,0:T(8,128)(2,1)}, bf16[4,128,256]{2,1,0:T(8,128)(2,1)S(1)}, u32[]{:S(2)}) copy-start(bf16[4,128,256]{2,1,0:T(8,128)(2,1)S(1)} %get-tuple-element.56.refs_3_) | copy-start | bytes 786436 | tf_op jit(solution)/shard_map/cond
  22.8 45.1 %copy-start.38 = (bf16[4,128,256]{2,1,0:T(8,128)(2,1)}, bf16[4,128,256]{2,1,0:T(8,128)(2,1)S(1)}, u32[]{:S(2)}) copy-start(bf16[4,128,256]{2,1,0:T(8,128)(2,1)S(1)} %get-tuple-element.53.refs_0_) | copy-start | bytes 786436 | tf_op jit(solution)/shard_map/cond
  22.9 45.1 %copy-start.42 = (bf16[4,128,256]{2,1,0:T(8,128)(2,1)}, bf16[4,128,256]{2,1,0:T(8,128)(2,1)S(1)}, u32[]{:S(2)}) copy-start(bf16[4,128,256]{2,1,0:T(8,128)(2,1)S(1)} %get-tuple-element.54.refs_1_) | copy-start | bytes 786436 | tf_op jit(solution)/shard_map/cond
  25.2 76.0 %all-to-all-start = ((bf16[4,1024,256]{2,1,0:T(8,128)(2,1)}), bf16[4,1024,256]{2,1,0:T(8,128)(2,1)S(1)}, u32[]{:S(2)}, u32[]{:S(2)}) async-start(bf16[4,1024,256]{2,1,0:T(8,128)(2,1)} %give_contexts.2), calls=%async_computation | async-start | bytes 4194304 | tf_op jit(solution)/shard_map/cond/branch_0_fun/all_to_all | solution.py:483
  31.3 32.6 %collective-permute-start = (bf16[9,128,256]{2,1,0:T(8,128)(2,1)}, bf16[9,128,256]{2,1,0:T(8,128)(2,1)}, u32[]{:S(2)}, u32[]{:S(2)}) collective-permute-start(bf16[9,128,256]{2,1,0:T(8,128)(2,1)} %pick_lanes.4), channel_id=1, source_target_pairs={{0,4},{1,5},{2,6},{3,7},{4,0},{5,1},{6,2},{7,3},{8,12},{9,13},{10,... | collective-permute-start | bytes 1769480 | tf_op jit(solution)/shard_map/cond/branch_0_fun/ppermute | solution.py:22
  36.9 8.7 %collective-permute-start.11 = (bf16[4,128,256]{2,1,0:T(8,128)(2,1)}, bf16[4,128,256]{2,1,0:T(8,128)(2,1)S(1)}, u32[]{:S(2)}, u32[]{:S(2)}) collective-permute-start(bf16[4,128,256]{2,1,0:T(8,128)(2,1)} %get-tuple-element.77), channel_id=1, source_target_pairs={{0,1},{1,0},{2,3},{3,2},{4,5},{5,4},{6,7},{7,6},{8,9},{9,8},{10,11... | collective-permute-start | bytes 786440 | tf_op jit(solution)/shard_map/cond/branch_0_fun/ppermute | solution.py:22
  38.5 15.3 %collective-permute-start.12 = (bf16[4,128,256]{2,1,0:T(8,128)(2,1)}, bf16[4,128,256]{2,1,0:T(8,128)(2,1)S(1)}, u32[]{:S(2)}, u32[]{:S(2)}) collective-permute-start(bf16[4,128,256]{2,1,0:T(8,128)(2,1)} %get-tuple-element.78), channel_id=1, source_target_pairs={{0,2},{1,3},{2,0},{3,1},{4,6},{5,7},{6,4},{7,5},{8,10},{9,11},{10,... | collective-permute-start | bytes 786440 | tf_op jit(solution)/shard_map/cond/branch_0_fun/ppermute | solution.py:22
  40.1 23.8 %collective-permute-start.13 = (bf16[4,128,256]{2,1,0:T(8,128)(2,1)}, bf16[4,128,256]{2,1,0:T(8,128)(2,1)S(1)}, u32[]{:S(2)}, u32[]{:S(2)}) collective-permute-start(bf16[4,128,256]{2,1,0:T(8,128)(2,1)} %get-tuple-element.79), channel_id=1, source_target_pairs={{0,3},{1,2},{2,1},{3,0},{4,7},{5,6},{6,5},{7,4},{8,11},{9,10},{10,... | collective-permute-start | bytes 786440 | tf_op jit(solution)/shard_map/cond/branch_0_fun/ppermute | solution.py:22
  45.6 18.3 %copy-start.3 = (bf16[4,128,256]{2,1,0:T(8,128)(2,1)}, bf16[4,128,256]{2,1,0:T(8,128)(2,1)S(1)}, u32[]{:S(2)}) copy-start(bf16[4,128,256]{2,1,0:T(8,128)(2,1)S(1)} %collective-permute-done.11.refs_1_) | copy-start | bytes 786436 | tf_op jit(solution)/shard_map/cond
  53.8 10.1 %copy-start.5 = (bf16[4,128,256]{2,1,0:T(8,128)(2,1)}, bf16[4,128,256]{2,1,0:T(8,128)(2,1)S(1)}, u32[]{:S(2)}) copy-start(bf16[4,128,256]{2,1,0:T(8,128)(2,1)S(1)} %collective-permute-done.12.refs_2_) | copy-start | bytes 786436 | tf_op jit(solution)/shard_map/cond
  63.9 0.7 copy-start.7
  67.1 27.4 %collective-permute-start.14 = (bf16[9,128,256]{2,1,0:T(8,128)(2,1)}, bf16[9,128,256]{2,1,0:T(8,128)(2,1)}, u32[]{:S(2)}, u32[]{:S(2)}) collective-permute-start(bf16[9,128,256]{2,1,0:T(8,128)(2,1)} %pick_lanes.5), channel_id=1, source_target_pairs={{0,4},{1,5},{2,6},{3,7},{4,0},{5,1},{6,2},{7,3},{8,12},{9,13},{10,... | collective-permute-start | bytes 1769480 | tf_op jit(solution)/shard_map/cond/branch_0_fun/ppermute | solution.py:22
  71.2 28.5 %collective-permute-start.1 = (bf16[4,128,256]{2,1,0:T(8,128)(2,1)}, bf16[4,128,256]{2,1,0:T(8,128)(2,1)S(1)}, u32[]{:S(2)}, u32[]{:S(2)}) collective-permute-start(bf16[4,128,256]{2,1,0:T(8,128)(2,1)} %get-tuple-element.58), channel_id=1, source_target_pairs={{0,1},{1,0},{2,3},{3,2},{4,5},{5,4},{6,7},{7,6},{8,9},{9,8},{10,11... | collective-permute-start | bytes 786440 | tf_op jit(solution)/shard_map/cond/branch_0_fun/ppermute | solution.py:22
  72.1 29.2 %collective-permute-start.2 = (bf16[4,128,256]{2,1,0:T(8,128)(2,1)}, bf16[4,128,256]{2,1,0:T(8,128)(2,1)S(1)}, u32[]{:S(2)}, u32[]{:S(2)}) collective-permute-start(bf16[4,128,256]{2,1,0:T(8,128)(2,1)} %get-tuple-element.59), channel_id=1, source_target_pairs={{0,2},{1,3},{2,0},{3,1},{4,6},{5,7},{6,4},{7,5},{8,10},{9,11},{10,... | collective-permute-start | bytes 786440 | tf_op jit(solution)/shard_map/cond/branch_0_fun/ppermute | solution.py:22
  75.2 26.0 %collective-permute-start.3 = (bf16[4,128,256]{2,1,0:T(8,128)(2,1)}, bf16[4,128,256]{2,1,0:T(8,128)(2,1)}, u32[]{:S(2)}, u32[]{:S(2)}) collective-permute-start(bf16[4,128,256]{2,1,0:T(8,128)(2,1)} %get-tuple-element.60), channel_id=1, source_target_pairs={{0,3},{1,2},{2,1},{3,0},{4,7},{5,6},{6,5},{7,4},{8,11},{9,10},{10,... | collective-permute-start | bytes 786440 | tf_op jit(solution)/shard_map/cond/branch_0_fun/ppermute | solution.py:22
  97.5 16.0 %collective-permute-start.15 = (bf16[4,128,256]{2,1,0:T(8,128)(2,1)}, bf16[4,128,256]{2,1,0:T(8,128)(2,1)S(1)}, u32[]{:S(2)}, u32[]{:S(2)}) collective-permute-start(bf16[4,128,256]{2,1,0:T(8,128)(2,1)} %get-tuple-element.81), channel_id=1, source_target_pairs={{0,1},{1,0},{2,3},{3,2},{4,5},{5,4},{6,7},{7,6},{8,9},{9,8},{10,11... | collective-permute-start | bytes 786440 | tf_op jit(solution)/shard_map/cond/branch_0_fun/ppermute | solution.py:22
  99.7 17.2 %collective-permute-start.16 = (bf16[4,128,256]{2,1,0:T(8,128)(2,1)}, bf16[4,128,256]{2,1,0:T(8,128)(2,1)S(1)}, u32[]{:S(2)}, u32[]{:S(2)}) collective-permute-start(bf16[4,128,256]{2,1,0:T(8,128)(2,1)} %get-tuple-element.82), channel_id=1, source_target_pairs={{0,2},{1,3},{2,0},{3,1},{4,6},{5,7},{6,4},{7,5},{8,10},{9,11},{10,... | collective-permute-start | bytes 786440 | tf_op jit(solution)/shard_map/cond/branch_0_fun/ppermute | solution.py:22
  99.7 17.2 %collective-permute-start.17 = (bf16[4,128,256]{2,1,0:T(8,128)(2,1)}, bf16[4,128,256]{2,1,0:T(8,128)(2,1)S(1)}, u32[]{:S(2)}, u32[]{:S(2)}) collective-permute-start(bf16[4,128,256]{2,1,0:T(8,128)(2,1)} %get-tuple-element.83), channel_id=1, source_target_pairs={{0,3},{1,2},{2,1},{3,0},{4,7},{5,6},{6,5},{7,4},{8,11},{9,10},{10,... | collective-permute-start | bytes 786440 | tf_op jit(solution)/shard_map/cond/branch_0_fun/ppermute | solution.py:22
  101.2 1.0 copy-start.21
  102.2 14.7 %copy-start.20 = (bf16[4,128,256]{2,1,0:T(8,128)(2,1)S(1)}, bf16[4,128,256]{2,1,0:T(8,128)(2,1)}, u32[]{:S(2)}) copy-start(bf16[4,128,256]{2,1,0:T(8,128)(2,1)} %get-tuple-element.80.refs_0_) | copy-start | bytes 786436 | tf_op jit(solution)/shard_map/cond
  112.7 0.7 copy-start.28
  113.4 20.9 %collective-permute-start.4 = (bf16[4,128,256]{2,1,0:T(8,128)(2,1)}, bf16[4,128,256]{2,1,0:T(8,128)(2,1)S(1)}, u32[]{:S(2)}, u32[]{:S(2)}) collective-permute-start(bf16[4,128,256]{2,1,0:T(8,128)(2,1)} %get-tuple-element.66), channel_id=1, source_target_pairs={{0,1},{1,0},{2,3},{3,2},{4,5},{5,4},{6,7},{7,6},{8,9},{9,8},{10,11... | collective-permute-start | bytes 786440 | tf_op jit(solution)/shard_map/cond/branch_0_fun/ppermute | solution.py:22
  113.5 20.8 %collective-permute-start.5 = (bf16[4,128,256]{2,1,0:T(8,128)(2,1)}, bf16[4,128,256]{2,1,0:T(8,128)(2,1)}, u32[]{:S(2)}, u32[]{:S(2)}) collective-permute-start(bf16[4,128,256]{2,1,0:T(8,128)(2,1)} %get-tuple-element.67), channel_id=1, source_target_pairs={{0,2},{1,3},{2,0},{3,1},{4,6},{5,7},{6,4},{7,5},{8,10},{9,11},{10,... | collective-permute-start | bytes 786440 | tf_op jit(solution)/shard_map/cond/branch_0_fun/ppermute | solution.py:22
  113.5 20.8 %collective-permute-start.6 = (bf16[4,128,256]{2,1,0:T(8,128)(2,1)}, bf16[4,128,256]{2,1,0:T(8,128)(2,1)}, u32[]{:S(2)}, u32[]{:S(2)}) collective-permute-start(bf16[4,128,256]{2,1,0:T(8,128)(2,1)} %get-tuple-element.68), channel_id=1, source_target_pairs={{0,3},{1,2},{2,1},{3,0},{4,7},{5,6},{6,5},{7,4},{8,11},{9,10},{10,... | collective-permute-start | bytes 786440 | tf_op jit(solution)/shard_map/cond/branch_0_fun/ppermute | solution.py:22
  127.1 1.3 copy-start.16
  128.4 0.7 copy-start.30
  130.5 3.8 %copy-start.29 = (bf16[4,128,256]{2,1,0:T(8,128)(2,1)S(1)}, bf16[4,128,256]{2,1,0:T(8,128)(2,1)}, u32[]{:S(2)}) copy-start(bf16[4,128,256]{2,1,0:T(8,128)(2,1)} %copy-done.28) | copy-start | bytes 786436 | tf_op jit(solution)/shard_map/cond
  130.5 6.7 %copy-start.33 = (bf16[4,128,256]{2,1,0:T(8,128)(2,1)S(1)}, bf16[4,128,256]{2,1,0:T(8,128)(2,1)}, u32[]{:S(2)}) copy-start(bf16[4,128,256]{2,1,0:T(8,128)(2,1)} %copy-done.32) | copy-start | bytes 786436 | tf_op jit(solution)/shard_map/cond
  130.5 7.2 %copy-start.31 = (bf16[4,128,256]{2,1,0:T(8,128)(2,1)S(1)}, bf16[4,128,256]{2,1,0:T(8,128)(2,1)}, u32[]{:S(2)}) copy-start(bf16[4,128,256]{2,1,0:T(8,128)(2,1)} %copy-done.30) | copy-start | bytes 786436 | tf_op jit(solution)/shard_map/cond
  130.5 69.1 %all-to-all-start.1 = ((bf16[4,1024,256]{2,1,0:T(8,128)(2,1)}), bf16[4,1024,256]{2,1,0:T(8,128)(2,1)S(1)}, u32[]{:S(2)}, u32[]{:S(2)}) async-start(bf16[4,1024,256]{2,1,0:T(8,128)(2,1)} %copy-done.16), calls=%async_computation.1 | async-start | bytes 4194304 | tf_op jit(solution)/shard_map/cond/branch_0_fun/all_to_all | solution.py:498
  134.3 31.5 %copy-start.39 = (bf16[4,128,256]{2,1,0:T(8,128)(2,1)S(1)}, bf16[4,128,256]{2,1,0:T(8,128)(2,1)}, u32[]{:S(2)}) copy-start(bf16[4,128,256]{2,1,0:T(8,128)(2,1)} %copy-done.38) | copy-start | bytes 786436 | tf_op jit(solution)/shard_map/cond
  134.3 31.5 %copy-start.43 = (bf16[4,128,256]{2,1,0:T(8,128)(2,1)S(1)}, bf16[4,128,256]{2,1,0:T(8,128)(2,1)}, u32[]{:S(2)}) copy-start(bf16[4,128,256]{2,1,0:T(8,128)(2,1)} %copy-done.42) | copy-start | bytes 786436 | tf_op jit(solution)/shard_map/cond
  134.3 31.5 %copy-start.47 = (bf16[4,128,256]{2,1,0:T(8,128)(2,1)S(1)}, bf16[4,128,256]{2,1,0:T(8,128)(2,1)}, u32[]{:S(2)}) copy-start(bf16[4,128,256]{2,1,0:T(8,128)(2,1)} %copy-done.46) | copy-start | bytes 786436 | tf_op jit(solution)/shard_map/cond
  134.3 31.5 %copy-start.50 = (bf16[4,128,256]{2,1,0:T(8,128)(2,1)S(1)}, bf16[4,128,256]{2,1,0:T(8,128)(2,1)}, u32[]{:S(2)}) copy-start(bf16[4,128,256]{2,1,0:T(8,128)(2,1)} %copy-done.49) | copy-start | bytes 786436 | tf_op jit(solution)/shard_map/cond
  136.1 28.3 %collective-permute-start.7 = (bf16[9,128,256]{2,1,0:T(8,128)(2,1)S(1)}, bf16[9,128,256]{2,1,0:T(8,128)(2,1)S(1)}, u32[]{:S(2)}, u32[]{:S(2)}) collective-permute-start(bf16[9,128,256]{2,1,0:T(8,128)(2,1)S(1)} %get-tuple-element.70), channel_id=1, source_target_pairs={{0,4},{1,5},{2,6},{3,7},{4,0},{5,1},{6,2},{7,3},{8,12},{9,13},{10,... | collective-permute-start | bytes 1769480 | tf_op jit(solution)/shard_map/cond/branch_0_fun/ppermute | solution.py:22
  136.7 8.6 %collective-permute-start.18 = (bf16[4,128,256]{2,1,0:T(8,128)(2,1)}, bf16[4,128,256]{2,1,0:T(8,128)(2,1)S(1)}, u32[]{:S(2)}, u32[]{:S(2)}) collective-permute-start(bf16[4,128,256]{2,1,0:T(8,128)(2,1)} %copy-done.34), channel_id=1, source_target_pairs={{0,1},{1,0},{2,3},{3,2},{4,5},{5,4},{6,7},{7,6},{8,9},{9,8},{10,11... | collective-permute-start | bytes 786440 | tf_op jit(solution)/shard_map/cond/branch_0_fun/ppermute | solution.py:22
  137.2 18.8 %collective-permute-start.19 = (bf16[4,128,256]{2,1,0:T(8,128)(2,1)S(1)}, bf16[4,128,256]{2,1,0:T(8,128)(2,1)S(1)}, u32[]{:S(2)}, u32[]{:S(2)}) collective-permute-start(bf16[4,128,256]{2,1,0:T(8,128)(2,1)S(1)} %copy-done.33), channel_id=1, source_target_pairs={{0,2},{1,3},{2,0},{3,1},{4,6},{5,7},{6,4},{7,5},{8,10},{9,11},{10,... | collective-permute-start | bytes 786440 | tf_op jit(solution)/shard_map/cond/branch_0_fun/ppermute | solution.py:22
  137.7 23.5 %collective-permute-start.20 = (bf16[4,128,256]{2,1,0:T(8,128)(2,1)S(1)}, bf16[4,128,256]{2,1,0:T(8,128)(2,1)S(1)}, u32[]{:S(2)}, u32[]{:S(2)}) collective-permute-start(bf16[4,128,256]{2,1,0:T(8,128)(2,1)S(1)} %copy-done.31), channel_id=1, source_target_pairs={{0,3},{1,2},{2,1},{3,0},{4,7},{5,6},{6,5},{7,4},{8,11},{9,10},{10,... | collective-permute-start | bytes 786440 | tf_op jit(solution)/shard_map/cond/branch_0_fun/ppermute | solution.py:22
  165.6 28.1 %copy-start.2 = (bf16[4,128,256]{2,1,0:T(8,128)(2,1)S(1)}, bf16[4,128,256]{2,1,0:T(8,128)(2,1)}, u32[]{:S(2)}) copy-start(bf16[4,128,256]{2,1,0:T(8,128)(2,1)} %get-tuple-element.76.refs_0_) | copy-start | bytes 786436 | tf_op jit(solution)/shard_map/cond
  165.6 28.1 %copy-start.4 = (bf16[4,128,256]{2,1,0:T(8,128)(2,1)S(1)}, bf16[4,128,256]{2,1,0:T(8,128)(2,1)}, u32[]{:S(2)}) copy-start(bf16[4,128,256]{2,1,0:T(8,128)(2,1)} %copy-done.3) | copy-start | bytes 786436 | tf_op jit(solution)/shard_map/cond
  165.6 28.1 %copy-start.6 = (bf16[4,128,256]{2,1,0:T(8,128)(2,1)S(1)}, bf16[4,128,256]{2,1,0:T(8,128)(2,1)}, u32[]{:S(2)}) copy-start(bf16[4,128,256]{2,1,0:T(8,128)(2,1)} %copy-done.5) | copy-start | bytes 786436 | tf_op jit(solution)/shard_map/cond
  165.6 28.1 %copy-start.8 = (bf16[4,128,256]{2,1,0:T(8,128)(2,1)S(1)}, bf16[4,128,256]{2,1,0:T(8,128)(2,1)}, u32[]{:S(2)}) copy-start(bf16[4,128,256]{2,1,0:T(8,128)(2,1)} %copy-done.7) | copy-start | bytes 786436 | tf_op jit(solution)/shard_map/cond
  165.6 28.0 %collective-permute-start.21 = (bf16[9,128,256]{2,1,0:T(8,128)(2,1)S(1)}, bf16[9,128,256]{2,1,0:T(8,128)(2,1)S(1)}, u32[]{:S(2)}, u32[]{:S(2)}) collective-permute-start(bf16[9,128,256]{2,1,0:T(8,128)(2,1)S(1)} %get-tuple-element.90), channel_id=1, source_target_pairs={{0,4},{1,5},{2,6},{3,7},{4,0},{5,1},{6,2},{7,3},{8,12},{9,13},{10,... | collective-permute-start | bytes 1769480 | tf_op jit(solution)/shard_map/cond/branch_0_fun/ppermute | solution.py:22
  166.8 29.4 %copy-start.24 = (bf16[4,128,256]{2,1,0:T(8,128)(2,1)}, bf16[4,128,256]{2,1,0:T(8,128)(2,1)S(1)}, u32[]{:S(2)}) copy-start(bf16[4,128,256]{2,1,0:T(8,128)(2,1)S(1)} %get-tuple-element.71.refs_0_) | copy-start | bytes 786436 | tf_op jit(solution)/shard_map/cond
  166.8 29.4 %collective-permute-start.8 = (bf16[4,128,256]{2,1,0:T(8,128)(2,1)S(1)}, bf16[4,128,256]{2,1,0:T(8,128)(2,1)S(1)}, u32[]{:S(2)}, u32[]{:S(2)}) collective-permute-start(bf16[4,128,256]{2,1,0:T(8,128)(2,1)S(1)} %get-tuple-element.72), channel_id=1, source_target_pairs={{0,1},{1,0},{2,3},{3,2},{4,5},{5,4},{6,7},{7,6},{8,9},{9,8},{10,11... | collective-permute-start | bytes 786440 | tf_op jit(solution)/shard_map/cond/branch_0_fun/ppermute | solution.py:22
  168.3 36.4 %collective-permute-start.9 = (bf16[4,128,256]{2,1,0:T(8,128)(2,1)S(1)}, bf16[4,128,256]{2,1,0:T(8,128)(2,1)}, u32[]{:S(2)}, u32[]{:S(2)}) collective-permute-start(bf16[4,128,256]{2,1,0:T(8,128)(2,1)S(1)} %get-tuple-element.73), channel_id=1, source_target_pairs={{0,2},{1,3},{2,0},{3,1},{4,6},{5,7},{6,4},{7,5},{8,10},{9,11},{10,... | collective-permute-start | bytes 786440 | tf_op jit(solution)/shard_map/cond/branch_0_fun/ppermute | solution.py:22
  169.4 35.3 %collective-permute-start.10 = (bf16[4,128,256]{2,1,0:T(8,128)(2,1)S(1)}, bf16[4,128,256]{2,1,0:T(8,128)(2,1)}, u32[]{:S(2)}, u32[]{:S(2)}) collective-permute-start(bf16[4,128,256]{2,1,0:T(8,128)(2,1)S(1)} %get-tuple-element.74), channel_id=1, source_target_pairs={{0,3},{1,2},{2,1},{3,0},{4,7},{5,6},{6,5},{7,4},{8,11},{9,10},{10,... | collective-permute-start | bytes 786440 | tf_op jit(solution)/shard_map/cond/branch_0_fun/ppermute | solution.py:22
  194.7 0.7 copy-start.26
  195.4 9.3 %collective-permute-start.22 = (bf16[4,128,256]{2,1,0:T(8,128)(2,1)S(1)}, bf16[4,128,256]{2,1,0:T(8,128)(2,1)}, u32[]{:S(2)}, u32[]{:S(2)}) collective-permute-start(bf16[4,128,256]{2,1,0:T(8,128)(2,1)S(1)} %get-tuple-element.92), channel_id=1, source_target_pairs={{0,1},{1,0},{2,3},{3,2},{4,5},{5,4},{6,7},{7,6},{8,9},{9,8},{10,11... | collective-permute-start | bytes 786440 | tf_op jit(solution)/shard_map/cond/branch_0_fun/ppermute | solution.py:22
  196.2 9.3 %collective-permute-start.23 = (bf16[4,128,256]{2,1,0:T(8,128)(2,1)S(1)}, bf16[4,128,256]{2,1,0:T(8,128)(2,1)}, u32[]{:S(2)}, u32[]{:S(2)}) collective-permute-start(bf16[4,128,256]{2,1,0:T(8,128)(2,1)S(1)} %get-tuple-element.93), channel_id=1, source_target_pairs={{0,2},{1,3},{2,0},{3,1},{4,6},{5,7},{6,4},{7,5},{8,10},{9,11},{10,... | collective-permute-start | bytes 786440 | tf_op jit(solution)/shard_map/cond/branch_0_fun/ppermute | solution.py:22
  196.2 0.7 copy-start.52
  196.9 13.7 %collective-permute-start.24 = (bf16[4,128,256]{2,1,0:T(8,128)(2,1)S(1)}, bf16[4,128,256]{2,1,0:T(8,128)(2,1)}, u32[]{:S(2)}, u32[]{:S(2)}) collective-permute-start(bf16[4,128,256]{2,1,0:T(8,128)(2,1)S(1)} %get-tuple-element.94), channel_id=1, source_target_pairs={{0,3},{1,2},{2,1},{3,0},{4,7},{5,6},{6,5},{7,4},{8,11},{9,10},{10,... | collective-permute-start | bytes 786440 | tf_op jit(solution)/shard_map/cond/branch_0_fun/ppermute | solution.py:22
  (2 other events, 1.4 us)
where the time goes:
time: 215 us; the launch traced here: 214 us
  waiting for transfers between devices  102 us (47%)
  Pallas kernels  55.9 us (26%)
  starting transfers between devices  44 us (20%)
  local copies, waits for them, and re-layouts  10.1 us (5%)
    ppermute x31, waiting for transfers between devices, swap(): return lax.ppermute(x, axis, [(i, i ^ shift) for i in range(size)])  102 us
    ppermute x31, starting transfers between devices, swap(): return lax.ppermute(x, axis, [(i, i ^ shift) for i in range(size)])  36.7 us
    pallas_call x2, Pallas kernels, tile_step(): pl.pallas_call(functools.partial(tile_kernel, z, first, last, len(after))...  20.7 us
    cond x58, local copies, waits for them, and re-layouts  7.21 us
    pallas_call x2, Pallas kernels, pick_asked(): pl.pallas_call(functools.partial(asked_kernel, z, cap), out_shape=[jax.Sh...  6.23 us
    pallas_call x2, Pallas kernels, split_words(): pl.pallas_call(functools.partial(split_kernel, z, k), out_shape=[jax.Shap...  5.4 us
    pallas_call x1, Pallas kernels, context_step(): pl.pallas_call(functools.partial(context_kernel, z), out_shape=jax.ShapeD...  5.09 us
    pallas_call x2, Pallas kernels, pick_lanes(): pl.pallas_call(functools.partial(lanes_kernel, z, cap), out_shape=jax.Sha...  4.97 us
  transfers between devices with their start and end apart: 33, of which 14 were waited for; matrix products, arithmetic and copies ran while one was open for 1% of the time, Pallas kernels for 23%

commit v1 on v0

--- a/solution.py
+++ b/solution.py
@@ -474,12 +474,13 @@
         ]
     ).astype(i32)
 
+    outgoing = give_contexts(z, info, contexts, [])
+
     def exchange(pieces):
         return [pieces[0]] + [swap(pieces[s], "col", s) for s in range(1, z.half)]
 
     def rest(cap):
-        def run(pool_0, table):
-            outgoing = give_contexts(z, info, contexts, [])
+        def run(pool_0, table, outgoing):
             ctx_tiles = lax.all_to_all(outgoing, "row", 0, 0, tiled=True)
             pools = [list(pool_0)] + [spread(k, []) for k in range(1, chunks)]
             so_far, lanes, asked, made, own, returned, pieces = None, [], [], [], [], [], []
@@ -512,7 +513,7 @@
 
     caps = sorted({max(1, z.pool * n // 16) for n in (9, 16)})
     level = sum((table[0] > cap).astype(i32) for cap in caps[:-1])
-    new_words, new_contexts = lax.switch(level, [rest(cap) for cap in caps], tuple(pool_0), table)
+    new_words, new_contexts = lax.switch(level, [rest(cap) for cap in caps], tuple(pool_0), table, outgoing)
     return new_words[:, None], new_contexts[:, None]
 
 

time: 215 us -> 214 us (level)
  transfers between devices with their start and end apart: 33 -> 33, of which waited for: 14 -> 12; matrix products, arithmetic and copies ran while one was open for 1% -> 1% of each run, Pallas kernels for 23% -> 24%
where the time goes in v1:
time: 214 us
  waiting for transfers between devices  100 us (47%)
  Pallas kernels  55.8 us (26%)
  starting transfers between devices  44 us (21%)
  local copies, waits for them, and re-layouts  11.3 us (5%)
    ppermute x31, waiting for transfers between devices, swap(): return lax.ppermute(x, axis, [(i, i ^ shift) for i in range(size)])  100 us
    ppermute x31, starting transfers between devices, swap(): return lax.ppermute(x, axis, [(i, i ^ shift) for i in range(size)])  36.7 us
    pallas_call x2, Pallas kernels, tile_step(): pl.pallas_call(functools.partial(tile_kernel, z, first, last, len(after))...  20.7 us
    cond x58, local copies, waits for them, and re-layouts  8.51 us
    pallas_call x2, Pallas kernels, pick_asked(): pl.pallas_call(functools.partial(asked_kernel, z, cap), out_shape=[jax.Sh...  6.27 us
    pallas_call x2, Pallas kernels, split_words(): pl.pallas_call(functools.partial(split_kernel, z, k), out_shape=[jax.Shap...  5.41 us
    pallas_call x1, Pallas kernels, context_step(): pl.pallas_call(functools.partial(context_kernel, z), out_shape=jax.ShapeD...  5.09 us
    pallas_call x2, Pallas kernels, pick_lanes(): pl.pallas_call(functools.partial(lanes_kernel, z, cap), out_shape=jax.Sha...  4.97 us
  transfers between devices with their start and end apart: 33, of which 12 were waited for; matrix products, arithmetic and copies ran while one was open for 1% of the time, Pallas kernels for 24%

profile of v1, /device:TPU:0, one launch (start us, length us, event | category | flops | bytes accessed | tf_op | source)
XLA Modules:
  0.0 213.9 jit_solution(3666929808054466631)
XLA Ops:
  0.7 0.8 copy.17
  1.5 2.4 %collective-permute-start.52 = (s32[1,32]{1,0:T(1,128)S(1)}, s32[1,32]{1,0:T(1,128)S(1)}, u32[]{:S(2)}, u32[]{:S(2)}) collective-permute-start(s32[1,32]{1,0:T(1,128)S(1)} %reshape.15), channel_id=1, source_target_pairs={{0,24},{8,16},{16,8},{24,0},{1,25},{9,17},{17,9},{25,1},{2,26},{10... | collective-permute-start | bytes 392 | tf_op jit(solution)/shard_map/ppermute | solution.py:22
  3.9 0.6 collective-permute-start.51
  4.6 2.6 %split_words.5 = (bf16[4,128,256]{2,1,0:T(8,128)(2,1)S(1)}, bf16[4,128,256]{2,1,0:T(8,128)(2,1)}, bf16[4,128,256]{2,1,0:T(8,128)(2,1)}, bf16[4,128,256]{2,1,0:T(8,128)(2,1)}) custom-call(s32[2]{0:T(128)S(1)} %pad_add_fusion.1.me_ref, bf16[4,1024,256]{2,1,0:T(8,128)(2,1)} %bitcast.34), custom_call_target="tpu_custom_call" | custom-call | tf_op jit(solution)/shard_map/split_words/pallas_call | solution.py:146
  7.2 1.6 collective-permute-start.53
  8.8 1.6 collective-permute-start.54
  11.0 1.3 dynamic_slice.7
  12.3 0.6 broadcast_in_dim.19
  13.1 2.1 give_contexts.1
  15.2 0.6 pad_add_fusion.lists_ref
  15.8 2.8 %tables.1 = s32[72]{0:T(128)S(1)} custom-call(s32[2]{0:T(128)S(1)} %pad_add_fusion.1.me_ref, s32[4,32]{1,0:T(4,128)} %pad_add_fusion.lists_ref, s32[4,8]{1,0:T(4,128)} %count_ref.1), custom_call_target="tpu_custom_call" | custom-call | tf_op jit(solution)/shard_map/tables/pallas_call | solution.py:123
  18.7 4.0 %collective-permute-done.55 = bf16[4,128,256]{2,1,0:T(8,128)(2,1)S(1)} collective-permute-done((bf16[4,128,256]{2,1,0:T(8,128)(2,1)}, bf16[4,128,256]{2,1,0:T(8,128)(2,1)S(1)}, u32[]{:S(2)}, u32[]{:S(2)}) %collective-permute-start.55) | collective-permute-done | bytes 262176 | tf_op jit(solution)/shard_map/ppermute | solution.py:22
  22.7 191.0 %conditional.1 = (bf16[4,1,1024,256]{3,2,1,0:T(8,128)(2,1)}, bf16[4,1,1024,256]{3,2,1,0:T(8,128)(2,1)}) conditional(s32[]{:T(128)} %bitcast.14, (s32[72]{0:T(128)S(1)}, bf16[4,128,256]{2,1,0:T(8,128)(2,1)S(1)}, bf16[4,128,256]{2,1,0:T(8,128)(2,1)S(1)}, bf16[4,128,256]{2,1,0:T(8,128)(2,1)S(1)}, bf16[4,128,256]{2,1,0:T(8,128)(2,1)S(1)}, ...), branch_computations={%region_1.2_spmd, %region_2.3_spmd} | conditional | bytes 138413840 | solution.py:516
  22.7 1.3 copy-done.35
  24.0 3.6 %all-to-all-start = ((bf16[4,1024,256]{2,1,0:T(8,128)(2,1)}), bf16[4,1024,256]{2,1,0:T(8,128)(2,1)S(1)}, u32[]{:S(2)}, u32[]{:S(2)}) async-start(bf16[4,1024,256]{2,1,0:T(8,128)(2,1)} %copy-done.35), calls=%async_computation | async-start | bytes 4194304 | tf_op jit(solution)/shard_map/cond/branch_0_fun/all_to_all | solution.py:484
  27.7 2.4 %pick_lanes.4 = bf16[9,128,256]{2,1,0:T(8,128)(2,1)} custom-call(s32[72]{0:T(128)S(1)} %get-tuple-element.55.table_ref, bf16[4,128,256]{2,1,0:T(8,128)(2,1)S(1)} %get-tuple-element.57.refs_0_, bf16[4,128,256]{2,1,0:T(8,128)(2,1)S(1)} %get-tuple-element.58.refs_1_, bf16[4,128,256]{2,1,0:T(8,128)(2,1)S(1)} %get-tuple-element.59.refs_2_, ...), custom_call_target="tpu_custom_call" | custom-call | tf_op jit(solution)/shard_map/cond/branch_0_fun/pick_lanes/pallas_call | solution.py:172
  30.1 2.8 %collective-permute-start = (bf16[9,128,256]{2,1,0:T(8,128)(2,1)}, bf16[9,128,256]{2,1,0:T(8,128)(2,1)}, u32[]{:S(2)}, u32[]{:S(2)}) collective-permute-start(bf16[9,128,256]{2,1,0:T(8,128)(2,1)} %pick_lanes.4), channel_id=1, source_target_pairs={{0,4},{1,5},{2,6},{3,7},{4,0},{5,1},{6,2},{7,3},{8,12},{9,13},{10,... | collective-permute-start | bytes 1769480 | tf_op jit(solution)/shard_map/cond/branch_0_fun/ppermute | solution.py:22
  32.9 2.8 %split_words.3 = (bf16[4,128,256]{2,1,0:T(8,128)(2,1)}, bf16[4,128,256]{2,1,0:T(8,128)(2,1)}, bf16[4,128,256]{2,1,0:T(8,128)(2,1)}, bf16[4,128,256]{2,1,0:T(8,128)(2,1)}) custom-call(s32[2]{0:T(128)S(1)} %get-tuple-element.54.me_ref, bf16[4,1024,256]{2,1,0:T(8,128)(2,1)} %get-tuple-element.79.words_ref), custom_call_target="tpu_custom_call" | custom-call | tf_op jit(solution)/shard_map/cond/branch_0_fun/split_words/pallas_call | solution.py:146
  35.7 1.6 collective-permute-start.11
  37.3 1.6 collective-permute-start.12
  39.2 5.1 %collective-permute-done.11.refs_1_ = bf16[4,128,256]{2,1,0:T(8,128)(2,1)S(1)} collective-permute-done((bf16[4,128,256]{2,1,0:T(8,128)(2,1)}, bf16[4,128,256]{2,1,0:T(8,128)(2,1)S(1)}, u32[]{:S(2)}, u32[]{:S(2)}) %collective-permute-start.11) | collective-permute-done | bytes 262176 | tf_op jit(solution)/shard_map/cond/branch_0_fun/ppermute | solution.py:22
  44.3 8.2 %collective-permute-done.12.refs_2_ = bf16[4,128,256]{2,1,0:T(8,128)(2,1)S(1)} collective-permute-done((bf16[4,128,256]{2,1,0:T(8,128)(2,1)}, bf16[4,128,256]{2,1,0:T(8,128)(2,1)S(1)}, u32[]{:S(2)}, u32[]{:S(2)}) %collective-permute-start.12) | collective-permute-done | bytes 262176 | tf_op jit(solution)/shard_map/cond/branch_0_fun/ppermute | solution.py:22
  52.5 10.1 %collective-permute-done.13.refs_3_ = bf16[4,128,256]{2,1,0:T(8,128)(2,1)S(1)} collective-permute-done((bf16[4,128,256]{2,1,0:T(8,128)(2,1)}, bf16[4,128,256]{2,1,0:T(8,128)(2,1)S(1)}, u32[]{:S(2)}, u32[]{:S(2)}) %collective-permute-start.13) | collective-permute-done | bytes 262176 | tf_op jit(solution)/shard_map/cond/branch_0_fun/ppermute | solution.py:22
  62.7 0.7 copy-done.7
  63.4 2.5 %pick_lanes.5 = bf16[9,128,256]{2,1,0:T(8,128)(2,1)} custom-call(s32[72]{0:T(128)S(1)} %get-tuple-element.55.table_ref, bf16[4,128,256]{2,1,0:T(8,128)(2,1)} %get-tuple-element.80.refs_0_, bf16[4,128,256]{2,1,0:T(8,128)(2,1)} %copy-done.3, bf16[4,128,256]{2,1,0:T(8,128)(2,1)} %copy-done.5, bf16[4,128,256]{2,1,0:T(8,128)(2,1)} %copy-done.7, ...), custom_call_target="tpu_custom_call" | custom-call | tf_op jit(solution)/shard_map/cond/branch_0_fun/pick_lanes/pallas_call | solution.py:172
  65.9 0.7 collective-permute-start.14
  66.6 3.3 %pick_asked.4 = (bf16[4,128,256]{2,1,0:T(8,128)(2,1)}, bf16[4,128,256]{2,1,0:T(8,128)(2,1)}, bf16[4,128,256]{2,1,0:T(8,128)(2,1)}, bf16[4,128,256]{2,1,0:T(8,128)(2,1)}) custom-call(s32[72]{0:T(128)S(1)} %get-tuple-element.55.table_ref, bf16[4,128,256]{2,1,0:T(8,128)(2,1)S(1)} %get-tuple-element.57.refs_0_, ...), custom_call_target="tpu_custom_call" | custom-call | tf_op jit(solution)/shard_map/cond/branch_0_fun/pick_asked/pallas_call | solution.py:201
  69.9 0.9 collective-permute-start.1
  70.8 3.0 %collective-permute-start.2 = (bf16[4,128,256]{2,1,0:T(8,128)(2,1)}, bf16[4,128,256]{2,1,0:T(8,128)(2,1)S(1)}, u32[]{:S(2)}, u32[]{:S(2)}) collective-permute-start(bf16[4,128,256]{2,1,0:T(8,128)(2,1)} %get-tuple-element.63), channel_id=1, source_target_pairs={{0,2},{1,3},{2,0},{3,1},{4,6},{5,7},{6,4},{7,5},{8,10},{9,11},{10,... | collective-permute-start | bytes 786440 | tf_op jit(solution)/shard_map/cond/branch_0_fun/ppermute | solution.py:22
  73.8 19.5 %collective-permute-done.14.refs_4_ = bf16[9,128,256]{2,1,0:T(8,128)(2,1)} collective-permute-done((bf16[9,128,256]{2,1,0:T(8,128)(2,1)}, bf16[9,128,256]{2,1,0:T(8,128)(2,1)}, u32[]{:S(2)}, u32[]{:S(2)}) %collective-permute-start.14) | collective-permute-done | bytes 589856 | tf_op jit(solution)/shard_map/cond/branch_0_fun/ppermute | solution.py:22
  93.3 3.0 %pick_asked.5 = (bf16[4,128,256]{2,1,0:T(8,128)(2,1)}, bf16[4,128,256]{2,1,0:T(8,128)(2,1)}, bf16[4,128,256]{2,1,0:T(8,128)(2,1)}, bf16[4,128,256]{2,1,0:T(8,128)(2,1)}) custom-call(s32[72]{0:T(128)S(1)} %get-tuple-element.55.table_ref, bf16[4,128,256]{2,1,0:T(8,128)(2,1)} %get-tuple-element.80.refs_0_, bf16[4,128,256]{2,1,0:T(8,128)(2,1)} %copy-done.3, ...), custom_call_target="tpu_custom_call" | custom-call | tf_op jit(solution)/shard_map/cond/branch_0_fun/pick_asked/pallas_call | solution.py:201
  96.3 2.2 %collective-permute-start.15 = (bf16[4,128,256]{2,1,0:T(8,128)(2,1)}, bf16[4,128,256]{2,1,0:T(8,128)(2,1)S(1)}, u32[]{:S(2)}, u32[]{:S(2)}) collective-permute-start(bf16[4,128,256]{2,1,0:T(8,128)(2,1)} %get-tuple-element.85), channel_id=1, source_target_pairs={{0,1},{1,0},{2,3},{3,2},{4,5},{5,4},{6,7},{7,6},{8,9},{9,8},{10,11... | collective-permute-start | bytes 786440 | tf_op jit(solution)/shard_map/cond/branch_0_fun/ppermute | solution.py:22
  98.5 1.5 collective-permute-start.17
  100.0 0.9 copy-done.21
  101.0 10.5 %tile_step.4 = (bf16[4,128,256]{2,1,0:T(8,128)(2,1)S(1)}, bf16[4,128,256]{2,1,0:T(8,128)(2,1)}, bf16[4,128,256]{2,1,0:T(8,128)(2,1)}, bf16[4,128,256]{2,1,0:T(8,128)(2,1)}, f32[4,256,1024]{2,1,0:T(8,128)S(1)}) custom-call(s32[20]{0:T(128)S(1)} %get-tuple-element.56.info_ref, bf16[4,128,256]{2,1,0:T(8,128)(2,1)S(1)} %copy-done.21, ...), custom_call_target="tpu_custom_call" | custom-call | tf_op jit(solution)/shard_map/cond/branch_0_fun/tile_step/pallas_call | solution.py:297
  111.4 0.7 copy-done.28
  112.2 1.9 collective-permute-start.4
  114.1 1.5 collective-permute-start.6
  115.7 10.2 %tile_step.5 = (bf16[4,128,256]{2,1,0:T(8,128)(2,1)S(1)}, bf16[4,128,256]{2,1,0:T(8,128)(2,1)S(1)}, bf16[4,128,256]{2,1,0:T(8,128)(2,1)S(1)}, bf16[4,128,256]{2,1,0:T(8,128)(2,1)S(1)}, bf16[4,1024,256]{2,1,0:T(8,128)(2,1)S(1)}) custom-call(s32[20]{0:T(128)S(1)} %get-tuple-element.56.info_ref, bf16[4,128,256]{2,1,0:T(8,128)(2,1)S(1)} %copy-done.20, ...), custom_call_target="tpu_custom_call" | custom-call | tf_op jit(solution)/shard_map/cond/branch_0_fun/tile_step/pallas_call | solution.py:297
  125.9 1.3 copy-done.16
  127.2 0.7 copy-done.30
  127.9 0.7 copy-done.32
  128.6 0.7 copy-done.34
  129.3 3.7 %all-to-all-start.1 = ((bf16[4,1024,256]{2,1,0:T(8,128)(2,1)}), bf16[4,1024,256]{2,1,0:T(8,128)(2,1)S(1)}, u32[]{:S(2)}, u32[]{:S(2)}) async-start(bf16[4,1024,256]{2,1,0:T(8,128)(2,1)} %copy-done.16), calls=%async_computation.1 | async-start | bytes 4194304 | tf_op jit(solution)/shard_map/cond/branch_0_fun/all_to_all | solution.py:499
  133.1 1.8 sum_parts.4
  135.0 2.0 collective-permute-start.18
  137.3 1.5 collective-permute-start.20
  138.8 5.3 %collective-permute-done.18.refs_1_ = bf16[4,128,256]{2,1,0:T(8,128)(2,1)S(1)} collective-permute-done((bf16[4,128,256]{2,1,0:T(8,128)(2,1)}, bf16[4,128,256]{2,1,0:T(8,128)(2,1)S(1)}, u32[]{:S(2)}, u32[]{:S(2)}) %collective-permute-start.18) | collective-permute-done | bytes 262176 | tf_op jit(solution)/shard_map/cond/branch_0_fun/ppermute | solution.py:22
  144.1 10.2 %collective-permute-done.19.refs_2_ = bf16[4,128,256]{2,1,0:T(8,128)(2,1)S(1)} collective-permute-done((bf16[4,128,256]{2,1,0:T(8,128)(2,1)S(1)}, bf16[4,128,256]{2,1,0:T(8,128)(2,1)S(1)}, u32[]{:S(2)}, u32[]{:S(2)}) %collective-permute-start.19) | collective-permute-done | bytes 262176 | tf_op jit(solution)/shard_map/cond/branch_0_fun/ppermute | solution.py:22
  154.4 5.4 %collective-permute-done.20.refs_3_ = bf16[4,128,256]{2,1,0:T(8,128)(2,1)S(1)} collective-permute-done((bf16[4,128,256]{2,1,0:T(8,128)(2,1)S(1)}, bf16[4,128,256]{2,1,0:T(8,128)(2,1)S(1)}, u32[]{:S(2)}, u32[]{:S(2)}) %collective-permute-start.20) | collective-permute-done | bytes 262176 | tf_op jit(solution)/shard_map/cond/branch_0_fun/ppermute | solution.py:22
  159.7 3.7 %collective-permute-done.7.lanes_ref.refs_4_ = bf16[9,128,256]{2,1,0:T(8,128)(2,1)S(1)} collective-permute-done((bf16[9,128,256]{2,1,0:T(8,128)(2,1)S(1)}, bf16[9,128,256]{2,1,0:T(8,128)(2,1)S(1)}, u32[]{:S(2)}, u32[]{:S(2)}) %collective-permute-start.7) | collective-permute-done | bytes 589856 | tf_op jit(solution)/shard_map/cond/branch_0_fun/ppermute | solution.py:22
  163.4 1.2 sum_parts.5
  164.7 0.8 collective-permute-start.21
  165.6 1.0 word_step.4
  166.6 1.5 collective-permute-start.8
  168.0 2.2 %collective-permute-start.9 = (bf16[4,128,256]{2,1,0:T(8,128)(2,1)S(1)}, bf16[4,128,256]{2,1,0:T(8,128)(2,1)}, u32[]{:S(2)}, u32[]{:S(2)}) collective-permute-start(bf16[4,128,256]{2,1,0:T(8,128)(2,1)S(1)} %get-tuple-element.77), channel_id=1, source_target_pairs={{0,2},{1,3},{2,0},{3,1},{4,6},{5,7},{6,4},{7,5},{8,10},{9,11},{10,... | collective-permute-start | bytes 786440 | tf_op jit(solution)/shard_map/cond/branch_0_fun/ppermute | solution.py:22
  170.3 22.8 %collective-permute-done.21.lanes_ref = bf16[9,128,256]{2,1,0:T(8,128)(2,1)S(1)} collective-permute-done((bf16[9,128,256]{2,1,0:T(8,128)(2,1)S(1)}, bf16[9,128,256]{2,1,0:T(8,128)(2,1)S(1)}, u32[]{:S(2)}, u32[]{:S(2)}) %collective-permute-start.21) | collective-permute-done | bytes 589856 | tf_op jit(solution)/shard_map/cond/branch_0_fun/ppermute | solution.py:22
  193.1 1.0 word_step.5
  194.1 0.7 copy-done.26
  195.0 0.7 copy-done.51
  195.7 3.3 %collective-permute-start.24 = (bf16[4,128,256]{2,1,0:T(8,128)(2,1)S(1)}, bf16[4,128,256]{2,1,0:T(8,128)(2,1)}, u32[]{:S(2)}, u32[]{:S(2)}) collective-permute-start(bf16[4,128,256]{2,1,0:T(8,128)(2,1)S(1)} %get-tuple-element.98), channel_id=1, source_target_pairs={{0,3},{1,2},{2,1},{3,0},{4,7},{5,6},{6,5},{7,4},{8,11},{9,10},{10,... | collective-permute-start | bytes 786440 | tf_op jit(solution)/shard_map/cond/branch_0_fun/ppermute | solution.py:22
  199.0 5.1 %context_step.2 = bf16[4,1024,256]{2,1,0:T(8,128)(2,1)} custom-call(s32[20]{0:T(128)S(1)} %get-tuple-element.56.info_ref, bf16[4,1024,256]{2,1,0:T(8,128)(2,1)S(1)} %all-to-all-done.1.back_ref, bf16[4,1024,256]{2,1,0:T(8,128)(2,1)} %get-tuple-element.100.ctx_ref), custom_call_target="tpu_custom_call" | custom-call | tf_op jit(solution)/shard_map/cond/branch_0_fun/context_step/pallas_call | solution.py:426
  204.3 5.7 %collective-permute-done.24.refs_7_ = bf16[4,128,256]{2,1,0:T(8,128)(2,1)} collective-permute-done((bf16[4,128,256]{2,1,0:T(8,128)(2,1)S(1)}, bf16[4,128,256]{2,1,0:T(8,128)(2,1)}, u32[]{:S(2)}, u32[]{:S(2)}) %collective-permute-start.24) | collective-permute-done | bytes 262176 | tf_op jit(solution)/shard_map/cond/branch_0_fun/ppermute | solution.py:22
  210.0 3.4 %join_words.2 = bf16[4,1024,256]{2,1,0:T(8,128)(2,1)} custom-call(s32[2]{0:T(128)S(1)} %get-tuple-element.54.me_ref, bf16[4,128,256]{2,1,0:T(8,128)(2,1)} %copy-done.24, bf16[4,128,256]{2,1,0:T(8,128)(2,1)} %copy-done.51, bf16[4,128,256]{2,1,0:T(8,128)(2,1)} %collective-permute-done.9.refs_2_, bf16[4,128,256]{2,1,0:T(8,128)(2,1)} %collective-permute-done.10.refs_3_, ...), custom_call_target="tpu_custom_call" | custom-call | tf_op jit(solution)/shard_map/cond/branch_0_fun/join_words/pallas_call | solution.py:383
  (94 shorter events, 2.2 us)
Async XLA Ops:
  0.6 10.2 %copy-start.56 = (s32[4,1,4]{2,1,0:T(1,128)S(1)}, s32[4,1,4]{2,1,0:T(1,128)}, u32[]{:S(2)}) copy-start(s32[4,1,4]{2,1,0:T(1,128)} %param.13) | copy-start | bytes 196
  0.6 10.3 %copy-start.54 = (s32[1,1,4,1024]{3,2,1,0:T(4,128)S(1)}, s32[1,1,4,1024]{3,2,1,0:T(4,128)}, u32[]{:S(2)}) copy-start(s32[1,1,4,1024]{3,2,1,0:T(4,128)} %param.16) | copy-start | bytes 49156
  0.7 12.3 %copy-start.55 = (s32[1,1,4,1024]{3,2,1,0:T(4,128)S(1)}, s32[1,1,4,1024]{3,2,1,0:T(4,128)}, u32[]{:S(2)}) copy-start(s32[1,1,4,1024]{3,2,1,0:T(4,128)} %param.17) | copy-start | bytes 49156
  1.5 11.5 %collective-permute-start.52 = (s32[1,32]{1,0:T(1,128)S(1)}, s32[1,32]{1,0:T(1,128)S(1)}, u32[]{:S(2)}, u32[]{:S(2)}) collective-permute-start(s32[1,32]{1,0:T(1,128)S(1)} %reshape.15), channel_id=1, source_target_pairs={{0,24},{8,16},{16,8},{24,0},{1,25},{9,17},{17,9},{25,1},{2,26},{10... | collective-permute-start | bytes 392 | tf_op jit(solution)/shard_map/ppermute | solution.py:22
  3.9 11.3 %collective-permute-start.51 = (s32[1,32]{1,0:T(1,128)S(1)}, s32[1,32]{1,0:T(1,128)S(1)}, u32[]{:S(2)}, u32[]{:S(2)}) collective-permute-start(s32[1,32]{1,0:T(1,128)S(1)} %reshape.15), channel_id=1, source_target_pairs={{0,16},{8,24},{16,0},{24,8},{1,17},{9,25},{17,1},{25,9},{2,18},{10... | collective-permute-start | bytes 392 | tf_op jit(solution)/shard_map/ppermute | solution.py:22
  7.2 11.4 %collective-permute-start.53 = (bf16[4,128,256]{2,1,0:T(8,128)(2,1)}, bf16[4,128,256]{2,1,0:T(8,128)(2,1)S(1)}, u32[]{:S(2)}, u32[]{:S(2)}) collective-permute-start(bf16[4,128,256]{2,1,0:T(8,128)(2,1)} %get-tuple-element.155), channel_id=1, source_target_pairs={{0,1},{1,0},{2,3},{3,2},{4,5},{5,4},{6,7},{7,6},{8,9},{9,8},{10,11... | collective-permute-start | bytes 786440 | tf_op jit(solution)/shard_map/ppermute | solution.py:22
  8.8 9.8 %collective-permute-start.54 = (bf16[4,128,256]{2,1,0:T(8,128)(2,1)}, bf16[4,128,256]{2,1,0:T(8,128)(2,1)S(1)}, u32[]{:S(2)}, u32[]{:S(2)}) collective-permute-start(bf16[4,128,256]{2,1,0:T(8,128)(2,1)} %get-tuple-element.156), channel_id=1, source_target_pairs={{0,2},{1,3},{2,0},{3,1},{4,6},{5,7},{6,4},{7,5},{8,10},{9,11},{10,... | collective-permute-start | bytes 786440 | tf_op jit(solution)/shard_map/ppermute | solution.py:22
  10.4 12.3 %collective-permute-start.55 = (bf16[4,128,256]{2,1,0:T(8,128)(2,1)}, bf16[4,128,256]{2,1,0:T(8,128)(2,1)S(1)}, u32[]{:S(2)}, u32[]{:S(2)}) collective-permute-start(bf16[4,128,256]{2,1,0:T(8,128)(2,1)} %get-tuple-element.157), channel_id=1, source_target_pairs={{0,3},{1,2},{2,1},{3,0},{4,7},{5,6},{6,5},{7,4},{8,11},{9,10},{10,... | collective-permute-start | bytes 786440 | tf_op jit(solution)/shard_map/ppermute | solution.py:22
  13.0 2.2 %collective-permute-start.50 = (s32[1,32]{1,0:T(1,128)S(1)}, s32[1,32]{1,0:T(1,128)S(1)}, u32[]{:S(2)}, u32[]{:S(2)}) collective-permute-start(s32[1,32]{1,0:T(1,128)S(1)} %reshape.15), channel_id=1, source_target_pairs={{0,8},{8,0},{16,24},{24,16},{1,9},{9,1},{17,25},{25,17},{2,10},{10... | collective-permute-start | bytes 392 | tf_op jit(solution)/shard_map/ppermute | solution.py:22
  22.7 1.3 copy-start.35
  24.0 3.6 %copy-start.45 = (bf16[4,128,256]{2,1,0:T(8,128)(2,1)}, bf16[4,128,256]{2,1,0:T(8,128)(2,1)S(1)}, u32[]{:S(2)}) copy-start(bf16[4,128,256]{2,1,0:T(8,128)(2,1)S(1)} %get-tuple-element.59.refs_2_) | copy-start | bytes 786436 | tf_op jit(solution)/shard_map/cond
  24.0 3.6 %copy-start.48 = (bf16[4,128,256]{2,1,0:T(8,128)(2,1)}, bf16[4,128,256]{2,1,0:T(8,128)(2,1)S(1)}, u32[]{:S(2)}) copy-start(bf16[4,128,256]{2,1,0:T(8,128)(2,1)S(1)} %get-tuple-element.60.refs_3_) | copy-start | bytes 786436 | tf_op jit(solution)/shard_map/cond
  24.0 42.6 %copy-start.37 = (bf16[4,128,256]{2,1,0:T(8,128)(2,1)}, bf16[4,128,256]{2,1,0:T(8,128)(2,1)S(1)}, u32[]{:S(2)}) copy-start(bf16[4,128,256]{2,1,0:T(8,128)(2,1)S(1)} %get-tuple-element.57.refs_0_) | copy-start | bytes 786436 | tf_op jit(solution)/shard_map/cond
  24.0 42.6 %copy-start.41 = (bf16[4,128,256]{2,1,0:T(8,128)(2,1)}, bf16[4,128,256]{2,1,0:T(8,128)(2,1)S(1)}, u32[]{:S(2)}) copy-start(bf16[4,128,256]{2,1,0:T(8,128)(2,1)S(1)} %get-tuple-element.58.refs_1_) | copy-start | bytes 786436 | tf_op jit(solution)/shard_map/cond
  24.0 76.0 %all-to-all-start = ((bf16[4,1024,256]{2,1,0:T(8,128)(2,1)}), bf16[4,1024,256]{2,1,0:T(8,128)(2,1)S(1)}, u32[]{:S(2)}, u32[]{:S(2)}) async-start(bf16[4,1024,256]{2,1,0:T(8,128)(2,1)} %copy-done.35), calls=%async_computation | async-start | bytes 4194304 | tf_op jit(solution)/shard_map/cond/branch_0_fun/all_to_all | solution.py:484
  30.1 32.6 %collective-permute-start = (bf16[9,128,256]{2,1,0:T(8,128)(2,1)}, bf16[9,128,256]{2,1,0:T(8,128)(2,1)}, u32[]{:S(2)}, u32[]{:S(2)}) collective-permute-start(bf16[9,128,256]{2,1,0:T(8,128)(2,1)} %pick_lanes.4), channel_id=1, source_target_pairs={{0,4},{1,5},{2,6},{3,7},{4,0},{5,1},{6,2},{7,3},{8,12},{9,13},{10,... | collective-permute-start | bytes 1769480 | tf_op jit(solution)/shard_map/cond/branch_0_fun/ppermute | solution.py:22
  35.7 8.7 %collective-permute-start.11 = (bf16[4,128,256]{2,1,0:T(8,128)(2,1)}, bf16[4,128,256]{2,1,0:T(8,128)(2,1)S(1)}, u32[]{:S(2)}, u32[]{:S(2)}) collective-permute-start(bf16[4,128,256]{2,1,0:T(8,128)(2,1)} %get-tuple-element.81), channel_id=1, source_target_pairs={{0,1},{1,0},{2,3},{3,2},{4,5},{5,4},{6,7},{7,6},{8,9},{9,8},{10,11... | collective-permute-start | bytes 786440 | tf_op jit(solution)/shard_map/cond/branch_0_fun/ppermute | solution.py:22
  37.3 15.3 %collective-permute-start.12 = (bf16[4,128,256]{2,1,0:T(8,128)(2,1)}, bf16[4,128,256]{2,1,0:T(8,128)(2,1)S(1)}, u32[]{:S(2)}, u32[]{:S(2)}) collective-permute-start(bf16[4,128,256]{2,1,0:T(8,128)(2,1)} %get-tuple-element.82), channel_id=1, source_target_pairs={{0,2},{1,3},{2,0},{3,1},{4,6},{5,7},{6,4},{7,5},{8,10},{9,11},{10,... | collective-permute-start | bytes 786440 | tf_op jit(solution)/shard_map/cond/branch_0_fun/ppermute | solution.py:22
  38.8 23.8 %collective-permute-start.13 = (bf16[4,128,256]{2,1,0:T(8,128)(2,1)}, bf16[4,128,256]{2,1,0:T(8,128)(2,1)S(1)}, u32[]{:S(2)}, u32[]{:S(2)}) collective-permute-start(bf16[4,128,256]{2,1,0:T(8,128)(2,1)} %get-tuple-element.83), channel_id=1, source_target_pairs={{0,3},{1,2},{2,1},{3,0},{4,7},{5,6},{6,5},{7,4},{8,11},{9,10},{10,... | collective-permute-start | bytes 786440 | tf_op jit(solution)/shard_map/cond/branch_0_fun/ppermute | solution.py:22
  44.3 18.3 %copy-start.3 = (bf16[4,128,256]{2,1,0:T(8,128)(2,1)}, bf16[4,128,256]{2,1,0:T(8,128)(2,1)S(1)}, u32[]{:S(2)}) copy-start(bf16[4,128,256]{2,1,0:T(8,128)(2,1)S(1)} %collective-permute-done.11.refs_1_) | copy-start | bytes 786436 | tf_op jit(solution)/shard_map/cond
  52.5 10.2 %copy-start.5 = (bf16[4,128,256]{2,1,0:T(8,128)(2,1)}, bf16[4,128,256]{2,1,0:T(8,128)(2,1)S(1)}, u32[]{:S(2)}) copy-start(bf16[4,128,256]{2,1,0:T(8,128)(2,1)S(1)} %collective-permute-done.12.refs_2_) | copy-start | bytes 786436 | tf_op jit(solution)/shard_map/cond
  62.7 0.7 copy-start.7
  65.9 27.4 %collective-permute-start.14 = (bf16[9,128,256]{2,1,0:T(8,128)(2,1)}, bf16[9,128,256]{2,1,0:T(8,128)(2,1)}, u32[]{:S(2)}, u32[]{:S(2)}) collective-permute-start(bf16[9,128,256]{2,1,0:T(8,128)(2,1)} %pick_lanes.5), channel_id=1, source_target_pairs={{0,4},{1,5},{2,6},{3,7},{4,0},{5,1},{6,2},{7,3},{8,12},{9,13},{10,... | collective-permute-start | bytes 1769480 | tf_op jit(solution)/shard_map/cond/branch_0_fun/ppermute | solution.py:22
  69.9 28.5 %collective-permute-start.1 = (bf16[4,128,256]{2,1,0:T(8,128)(2,1)}, bf16[4,128,256]{2,1,0:T(8,128)(2,1)S(1)}, u32[]{:S(2)}, u32[]{:S(2)}) collective-permute-start(bf16[4,128,256]{2,1,0:T(8,128)(2,1)} %get-tuple-element.62), channel_id=1, source_target_pairs={{0,1},{1,0},{2,3},{3,2},{4,5},{5,4},{6,7},{7,6},{8,9},{9,8},{10,11... | collective-permute-start | bytes 786440 | tf_op jit(solution)/shard_map/cond/branch_0_fun/ppermute | solution.py:22
  70.8 29.2 %collective-permute-start.2 = (bf16[4,128,256]{2,1,0:T(8,128)(2,1)}, bf16[4,128,256]{2,1,0:T(8,128)(2,1)S(1)}, u32[]{:S(2)}, u32[]{:S(2)}) collective-permute-start(bf16[4,128,256]{2,1,0:T(8,128)(2,1)} %get-tuple-element.63), channel_id=1, source_target_pairs={{0,2},{1,3},{2,0},{3,1},{4,6},{5,7},{6,4},{7,5},{8,10},{9,11},{10,... | collective-permute-start | bytes 786440 | tf_op jit(solution)/shard_map/cond/branch_0_fun/ppermute | solution.py:22
  73.7 26.3 %collective-permute-start.3 = (bf16[4,128,256]{2,1,0:T(8,128)(2,1)}, bf16[4,128,256]{2,1,0:T(8,128)(2,1)}, u32[]{:S(2)}, u32[]{:S(2)}) collective-permute-start(bf16[4,128,256]{2,1,0:T(8,128)(2,1)} %get-tuple-element.64), channel_id=1, source_target_pairs={{0,3},{1,2},{2,1},{3,0},{4,7},{5,6},{6,5},{7,4},{8,11},{9,10},{10,... | collective-permute-start | bytes 786440 | tf_op jit(solution)/shard_map/cond/branch_0_fun/ppermute | solution.py:22
  96.3 17.9 %collective-permute-start.15 = (bf16[4,128,256]{2,1,0:T(8,128)(2,1)}, bf16[4,128,256]{2,1,0:T(8,128)(2,1)S(1)}, u32[]{:S(2)}, u32[]{:S(2)}) collective-permute-start(bf16[4,128,256]{2,1,0:T(8,128)(2,1)} %get-tuple-element.85), channel_id=1, source_target_pairs={{0,1},{1,0},{2,3},{3,2},{4,5},{5,4},{6,7},{7,6},{8,9},{9,8},{10,11... | collective-permute-start | bytes 786440 | tf_op jit(solution)/shard_map/cond/branch_0_fun/ppermute | solution.py:22
  98.5 17.2 %collective-permute-start.16 = (bf16[4,128,256]{2,1,0:T(8,128)(2,1)}, bf16[4,128,256]{2,1,0:T(8,128)(2,1)S(1)}, u32[]{:S(2)}, u32[]{:S(2)}) collective-permute-start(bf16[4,128,256]{2,1,0:T(8,128)(2,1)} %get-tuple-element.86), channel_id=1, source_target_pairs={{0,2},{1,3},{2,0},{3,1},{4,6},{5,7},{6,4},{7,5},{8,10},{9,11},{10,... | collective-permute-start | bytes 786440 | tf_op jit(solution)/shard_map/cond/branch_0_fun/ppermute | solution.py:22
  98.5 17.2 %collective-permute-start.17 = (bf16[4,128,256]{2,1,0:T(8,128)(2,1)}, bf16[4,128,256]{2,1,0:T(8,128)(2,1)S(1)}, u32[]{:S(2)}, u32[]{:S(2)}) collective-permute-start(bf16[4,128,256]{2,1,0:T(8,128)(2,1)} %get-tuple-element.87), channel_id=1, source_target_pairs={{0,3},{1,2},{2,1},{3,0},{4,7},{5,6},{6,5},{7,4},{8,11},{9,10},{10,... | collective-permute-start | bytes 786440 | tf_op jit(solution)/shard_map/cond/branch_0_fun/ppermute | solution.py:22
  100.0 1.0 copy-start.21
  101.0 14.7 %copy-start.20 = (bf16[4,128,256]{2,1,0:T(8,128)(2,1)S(1)}, bf16[4,128,256]{2,1,0:T(8,128)(2,1)}, u32[]{:S(2)}) copy-start(bf16[4,128,256]{2,1,0:T(8,128)(2,1)} %get-tuple-element.84.refs_0_) | copy-start | bytes 786436 | tf_op jit(solution)/shard_map/cond
  111.4 0.7 copy-start.28
  112.2 20.9 %collective-permute-start.4 = (bf16[4,128,256]{2,1,0:T(8,128)(2,1)}, bf16[4,128,256]{2,1,0:T(8,128)(2,1)S(1)}, u32[]{:S(2)}, u32[]{:S(2)}) collective-permute-start(bf16[4,128,256]{2,1,0:T(8,128)(2,1)} %get-tuple-element.70), channel_id=1, source_target_pairs={{0,1},{1,0},{2,3},{3,2},{4,5},{5,4},{6,7},{7,6},{8,9},{9,8},{10,11... | collective-permute-start | bytes 786440 | tf_op jit(solution)/shard_map/cond/branch_0_fun/ppermute | solution.py:22
  114.1 19.0 %collective-permute-start.5 = (bf16[4,128,256]{2,1,0:T(8,128)(2,1)}, bf16[4,128,256]{2,1,0:T(8,128)(2,1)}, u32[]{:S(2)}, u32[]{:S(2)}) collective-permute-start(bf16[4,128,256]{2,1,0:T(8,128)(2,1)} %get-tuple-element.71), channel_id=1, source_target_pairs={{0,2},{1,3},{2,0},{3,1},{4,6},{5,7},{6,4},{7,5},{8,10},{9,11},{10,... | collective-permute-start | bytes 786440 | tf_op jit(solution)/shard_map/cond/branch_0_fun/ppermute | solution.py:22
  114.1 19.0 %collective-permute-start.6 = (bf16[4,128,256]{2,1,0:T(8,128)(2,1)}, bf16[4,128,256]{2,1,0:T(8,128)(2,1)}, u32[]{:S(2)}, u32[]{:S(2)}) collective-permute-start(bf16[4,128,256]{2,1,0:T(8,128)(2,1)} %get-tuple-element.72), channel_id=1, source_target_pairs={{0,3},{1,2},{2,1},{3,0},{4,7},{5,6},{6,5},{7,4},{8,11},{9,10},{10,... | collective-permute-start | bytes 786440 | tf_op jit(solution)/shard_map/cond/branch_0_fun/ppermute | solution.py:22
  125.9 1.3 copy-start.16
  127.2 0.7 copy-start.30
  127.9 0.7 copy-start.32
  129.3 3.8 %copy-start.29 = (bf16[4,128,256]{2,1,0:T(8,128)(2,1)S(1)}, bf16[4,128,256]{2,1,0:T(8,128)(2,1)}, u32[]{:S(2)}) copy-start(bf16[4,128,256]{2,1,0:T(8,128)(2,1)} %copy-done.28) | copy-start | bytes 786436 | tf_op jit(solution)/shard_map/cond
  129.3 7.7 %copy-start.33 = (bf16[4,128,256]{2,1,0:T(8,128)(2,1)S(1)}, bf16[4,128,256]{2,1,0:T(8,128)(2,1)}, u32[]{:S(2)}) copy-start(bf16[4,128,256]{2,1,0:T(8,128)(2,1)} %copy-done.32) | copy-start | bytes 786436 | tf_op jit(solution)/shard_map/cond
  129.3 8.0 %copy-start.31 = (bf16[4,128,256]{2,1,0:T(8,128)(2,1)S(1)}, bf16[4,128,256]{2,1,0:T(8,128)(2,1)}, u32[]{:S(2)}) copy-start(bf16[4,128,256]{2,1,0:T(8,128)(2,1)} %copy-done.30) | copy-start | bytes 786436 | tf_op jit(solution)/shard_map/cond
  129.3 69.7 %all-to-all-start.1 = ((bf16[4,1024,256]{2,1,0:T(8,128)(2,1)}), bf16[4,1024,256]{2,1,0:T(8,128)(2,1)S(1)}, u32[]{:S(2)}, u32[]{:S(2)}) async-start(bf16[4,1024,256]{2,1,0:T(8,128)(2,1)} %copy-done.16), calls=%async_computation.1 | async-start | bytes 4194304 | tf_op jit(solution)/shard_map/cond/branch_0_fun/all_to_all | solution.py:499
  133.0 32.5 %copy-start.38 = (bf16[4,128,256]{2,1,0:T(8,128)(2,1)S(1)}, bf16[4,128,256]{2,1,0:T(8,128)(2,1)}, u32[]{:S(2)}) copy-start(bf16[4,128,256]{2,1,0:T(8,128)(2,1)} %copy-done.37) | copy-start | bytes 786436 | tf_op jit(solution)/shard_map/cond
  133.0 32.5 %copy-start.42 = (bf16[4,128,256]{2,1,0:T(8,128)(2,1)S(1)}, bf16[4,128,256]{2,1,0:T(8,128)(2,1)}, u32[]{:S(2)}) copy-start(bf16[4,128,256]{2,1,0:T(8,128)(2,1)} %copy-done.41) | copy-start | bytes 786436 | tf_op jit(solution)/shard_map/cond
  133.0 32.5 %copy-start.46 = (bf16[4,128,256]{2,1,0:T(8,128)(2,1)S(1)}, bf16[4,128,256]{2,1,0:T(8,128)(2,1)}, u32[]{:S(2)}) copy-start(bf16[4,128,256]{2,1,0:T(8,128)(2,1)} %copy-done.45) | copy-start | bytes 786436 | tf_op jit(solution)/shard_map/cond
  133.1 32.5 %copy-start.49 = (bf16[4,128,256]{2,1,0:T(8,128)(2,1)S(1)}, bf16[4,128,256]{2,1,0:T(8,128)(2,1)}, u32[]{:S(2)}) copy-start(bf16[4,128,256]{2,1,0:T(8,128)(2,1)} %copy-done.48) | copy-start | bytes 786436 | tf_op jit(solution)/shard_map/cond
  134.9 28.5 %collective-permute-start.7 = (bf16[9,128,256]{2,1,0:T(8,128)(2,1)S(1)}, bf16[9,128,256]{2,1,0:T(8,128)(2,1)S(1)}, u32[]{:S(2)}, u32[]{:S(2)}) collective-permute-start(bf16[9,128,256]{2,1,0:T(8,128)(2,1)S(1)} %get-tuple-element.74), channel_id=1, source_target_pairs={{0,4},{1,5},{2,6},{3,7},{4,0},{5,1},{6,2},{7,3},{8,12},{9,13},{10,... | collective-permute-start | bytes 1769480 | tf_op jit(solution)/shard_map/cond/branch_0_fun/ppermute | solution.py:22
  135.0 9.1 %collective-permute-start.18 = (bf16[4,128,256]{2,1,0:T(8,128)(2,1)}, bf16[4,128,256]{2,1,0:T(8,128)(2,1)S(1)}, u32[]{:S(2)}, u32[]{:S(2)}) collective-permute-start(bf16[4,128,256]{2,1,0:T(8,128)(2,1)} %copy-done.34), channel_id=1, source_target_pairs={{0,1},{1,0},{2,3},{3,2},{4,5},{5,4},{6,7},{7,6},{8,9},{9,8},{10,11... | collective-permute-start | bytes 786440 | tf_op jit(solution)/shard_map/cond/branch_0_fun/ppermute | solution.py:22
  137.0 17.4 %collective-permute-start.19 = (bf16[4,128,256]{2,1,0:T(8,128)(2,1)S(1)}, bf16[4,128,256]{2,1,0:T(8,128)(2,1)S(1)}, u32[]{:S(2)}, u32[]{:S(2)}) collective-permute-start(bf16[4,128,256]{2,1,0:T(8,128)(2,1)S(1)} %copy-done.33), channel_id=1, source_target_pairs={{0,2},{1,3},{2,0},{3,1},{4,6},{5,7},{6,4},{7,5},{8,10},{9,11},{10,... | collective-permute-start | bytes 786440 | tf_op jit(solution)/shard_map/cond/branch_0_fun/ppermute | solution.py:22
  137.3 22.4 %collective-permute-start.20 = (bf16[4,128,256]{2,1,0:T(8,128)(2,1)S(1)}, bf16[4,128,256]{2,1,0:T(8,128)(2,1)S(1)}, u32[]{:S(2)}, u32[]{:S(2)}) collective-permute-start(bf16[4,128,256]{2,1,0:T(8,128)(2,1)S(1)} %copy-done.31), channel_id=1, source_target_pairs={{0,3},{1,2},{2,1},{3,0},{4,7},{5,6},{6,5},{7,4},{8,11},{9,10},{10,... | collective-permute-start | bytes 786440 | tf_op jit(solution)/shard_map/cond/branch_0_fun/ppermute | solution.py:22
  164.7 28.4 %copy-start.2 = (bf16[4,128,256]{2,1,0:T(8,128)(2,1)S(1)}, bf16[4,128,256]{2,1,0:T(8,128)(2,1)}, u32[]{:S(2)}) copy-start(bf16[4,128,256]{2,1,0:T(8,128)(2,1)} %get-tuple-element.80.refs_0_) | copy-start | bytes 786436 | tf_op jit(solution)/shard_map/cond
  164.7 28.4 %copy-start.4 = (bf16[4,128,256]{2,1,0:T(8,128)(2,1)S(1)}, bf16[4,128,256]{2,1,0:T(8,128)(2,1)}, u32[]{:S(2)}) copy-start(bf16[4,128,256]{2,1,0:T(8,128)(2,1)} %copy-done.3) | copy-start | bytes 786436 | tf_op jit(solution)/shard_map/cond
  164.7 28.4 %copy-start.6 = (bf16[4,128,256]{2,1,0:T(8,128)(2,1)S(1)}, bf16[4,128,256]{2,1,0:T(8,128)(2,1)}, u32[]{:S(2)}) copy-start(bf16[4,128,256]{2,1,0:T(8,128)(2,1)} %copy-done.5) | copy-start | bytes 786436 | tf_op jit(solution)/shard_map/cond
  164.7 28.4 %copy-start.8 = (bf16[4,128,256]{2,1,0:T(8,128)(2,1)S(1)}, bf16[4,128,256]{2,1,0:T(8,128)(2,1)}, u32[]{:S(2)}) copy-start(bf16[4,128,256]{2,1,0:T(8,128)(2,1)} %copy-done.7) | copy-start | bytes 786436 | tf_op jit(solution)/shard_map/cond
  164.7 28.4 %collective-permute-start.21 = (bf16[9,128,256]{2,1,0:T(8,128)(2,1)S(1)}, bf16[9,128,256]{2,1,0:T(8,128)(2,1)S(1)}, u32[]{:S(2)}, u32[]{:S(2)}) collective-permute-start(bf16[9,128,256]{2,1,0:T(8,128)(2,1)S(1)} %get-tuple-element.94), channel_id=1, source_target_pairs={{0,4},{1,5},{2,6},{3,7},{4,0},{5,1},{6,2},{7,3},{8,12},{9,13},{10,... | collective-permute-start | bytes 1769480 | tf_op jit(solution)/shard_map/cond/branch_0_fun/ppermute | solution.py:22
  166.5 28.5 %copy-start.24 = (bf16[4,128,256]{2,1,0:T(8,128)(2,1)}, bf16[4,128,256]{2,1,0:T(8,128)(2,1)S(1)}, u32[]{:S(2)}) copy-start(bf16[4,128,256]{2,1,0:T(8,128)(2,1)S(1)} %get-tuple-element.75.refs_0_) | copy-start | bytes 786436 | tf_op jit(solution)/shard_map/cond
  166.6 28.5 %collective-permute-start.8 = (bf16[4,128,256]{2,1,0:T(8,128)(2,1)S(1)}, bf16[4,128,256]{2,1,0:T(8,128)(2,1)S(1)}, u32[]{:S(2)}, u32[]{:S(2)}) collective-permute-start(bf16[4,128,256]{2,1,0:T(8,128)(2,1)S(1)} %get-tuple-element.76), channel_id=1, source_target_pairs={{0,1},{1,0},{2,3},{3,2},{4,5},{5,4},{6,7},{7,6},{8,9},{9,8},{10,11... | collective-permute-start | bytes 786440 | tf_op jit(solution)/shard_map/cond/branch_0_fun/ppermute | solution.py:22
  168.0 36.1 %collective-permute-start.9 = (bf16[4,128,256]{2,1,0:T(8,128)(2,1)S(1)}, bf16[4,128,256]{2,1,0:T(8,128)(2,1)}, u32[]{:S(2)}, u32[]{:S(2)}) collective-permute-start(bf16[4,128,256]{2,1,0:T(8,128)(2,1)S(1)} %get-tuple-element.77), channel_id=1, source_target_pairs={{0,2},{1,3},{2,0},{3,1},{4,6},{5,7},{6,4},{7,5},{8,10},{9,11},{10,... | collective-permute-start | bytes 786440 | tf_op jit(solution)/shard_map/cond/branch_0_fun/ppermute | solution.py:22
  170.3 33.9 %collective-permute-start.10 = (bf16[4,128,256]{2,1,0:T(8,128)(2,1)S(1)}, bf16[4,128,256]{2,1,0:T(8,128)(2,1)}, u32[]{:S(2)}, u32[]{:S(2)}) collective-permute-start(bf16[4,128,256]{2,1,0:T(8,128)(2,1)S(1)} %get-tuple-element.78), channel_id=1, source_target_pairs={{0,3},{1,2},{2,1},{3,0},{4,7},{5,6},{6,5},{7,4},{8,11},{9,10},{10,... | collective-permute-start | bytes 786440 | tf_op jit(solution)/shard_map/cond/branch_0_fun/ppermute | solution.py:22
  194.1 0.7 copy-start.26
  194.8 9.3 %collective-permute-start.22 = (bf16[4,128,256]{2,1,0:T(8,128)(2,1)S(1)}, bf16[4,128,256]{2,1,0:T(8,128)(2,1)}, u32[]{:S(2)}, u32[]{:S(2)}) collective-permute-start(bf16[4,128,256]{2,1,0:T(8,128)(2,1)S(1)} %get-tuple-element.96), channel_id=1, source_target_pairs={{0,1},{1,0},{2,3},{3,2},{4,5},{5,4},{6,7},{7,6},{8,9},{9,8},{10,11... | collective-permute-start | bytes 786440 | tf_op jit(solution)/shard_map/cond/branch_0_fun/ppermute | solution.py:22
  195.0 9.3 %collective-permute-start.23 = (bf16[4,128,256]{2,1,0:T(8,128)(2,1)S(1)}, bf16[4,128,256]{2,1,0:T(8,128)(2,1)}, u32[]{:S(2)}, u32[]{:S(2)}) collective-permute-start(bf16[4,128,256]{2,1,0:T(8,128)(2,1)S(1)} %get-tuple-element.97), channel_id=1, source_target_pairs={{0,2},{1,3},{2,0},{3,1},{4,6},{5,7},{6,4},{7,5},{8,10},{9,11},{10,... | collective-permute-start | bytes 786440 | tf_op jit(solution)/shard_map/cond/branch_0_fun/ppermute | solution.py:22
  195.0 0.7 copy-start.51
  195.7 14.3 %collective-permute-start.24 = (bf16[4,128,256]{2,1,0:T(8,128)(2,1)S(1)}, bf16[4,128,256]{2,1,0:T(8,128)(2,1)}, u32[]{:S(2)}, u32[]{:S(2)}) collective-permute-start(bf16[4,128,256]{2,1,0:T(8,128)(2,1)S(1)} %get-tuple-element.98), channel_id=1, source_target_pairs={{0,3},{1,2},{2,1},{3,0},{4,7},{5,6},{6,5},{7,4},{8,11},{9,10},{10,... | collective-permute-start | bytes 786440 | tf_op jit(solution)/shard_map/cond/branch_0_fun/ppermute | solution.py:22
  (1 other events, 0.7 us)
